TPU v7x, 128 devices: a whole 4x4x4 slice. The times are simulated.
128 devices in a mesh: ctx: 32 (over y, z, core), ch: 4 (over x).
Axes of the slice: x: 4, y: 4, z: 4, core: 2. Of those that a mesh axis runs over, the one named last changes fastest.
Arguments:
- hyena_query: bfloat16 [4096, 4096], P('ctx', 'ch'), may hold values from -6 to 6
- hyena_key: bfloat16 [4096, 4096], P('ctx', 'ch'), may hold values from -6 to 6
- token_ids: int32 [4096], P('ctx'), may hold values from 0 to 511
- embed_table: bfloat16 [512, 4096], P(None, 'ch'), may hold values from -512 to 512
- norm_gain: float32 [4096], P('ch'), may hold values from 0.1 to 1.9
- hyena_filter: float32 [4096, 256], P('ctx', 'ch'), may hold values from -0.5 to 0.5
- attn_query: bfloat16 [4096, 4096], P('ctx', 'ch'), may hold values from -4.5 to 4.5
- attn_key: bfloat16 [4096, 4096], P('ctx', 'ch'), may hold values from -4.5 to 4.5
- document_ids: int32 [4096], P('ctx'), may hold values from 0 to 3, never falling along the last dimension, each value on 1 to 2048 neighbouring positions
Outputs:
- hyena_out: bfloat16 [4096, 4096], P('ctx', 'ch')
- attn_out: bfloat16 [4096, 4096], P('ctx', 'ch')
Inputs may be any that keep to these rules, and one draw needn't show every extreme that they name: `document_ids`: never falls along the sequence.
All inputs are finite; a program needn't handle non-finite values.
Results may differ from a plain program's by a relative error of at most 0.018.
Values may be sent and summed in bfloat16 or wider, within the bound.
A program may use at most 128 MiB of HBM per device.

v0:
```python
import math

import jax
import jax.numpy as jnp
from jax import lax
from jax.sharding import PartitionSpec as P

HEAD_DIM = 128


epsilon = 1e-06
masked_score = -1e30
highest = lax.Precision.HIGHEST


def from_partner(value, axis, distance):
    mask = 2**distance
    pairs = [(source, source ^ mask) for source in range(lax.axis_size(axis))]
    return lax.ppermute(value, axis, pairs)


def unit_angles(numerator, denominator):
    summed_result = (numerator % denominator).astype(jnp.float32)
    theta = summed_result * (2.0 * math.pi / denominator)
    return (jnp.cos(theta), jnp.sin(theta))


def rotate(values_now, cos_part, sin_part):
    real_part, imag_part = (values_now[:, 0], values_now[:, 1])
    return jnp.stack(
        [real_part * cos_part - imag_part * sin_part, imag_part * cos_part + real_part * sin_part],
        axis=1,
    )


def prepare(real_field, ctx_index, ctx_size):
    cos_part, sin_part = unit_angles(ctx_index, 2 * ctx_size)
    zero_field = jnp.zeros_like(real_field)
    plain = jnp.stack([real_field, zero_field])
    turned = jnp.stack([real_field * cos_part, -real_field * sin_part])
    return jnp.stack([plain, turned])


def forward_section(own_values, other_values, upper_half, cos_part, sin_part):
    lower_result = own_values + other_values
    upper_result = rotate(other_values - own_values, cos_part, -sin_part)
    return jnp.where(upper_half, upper_result, lower_result)


def inverse_section(own_values, other_values, upper_half, cos_part, sin_part):
    lower_result = own_values + rotate(other_values, cos_part, sin_part)
    upper_result = other_values - rotate(own_values, cos_part, sin_part)
    return jnp.where(upper_half, upper_result, lower_result)


def butterfly_forward(signal, taps_field, ctx_index, ctx_size):
    sections = ctx_size.bit_length() - 1
    for bit_index in reversed(range(sections)):
        half_span = 1 << bit_index
        other_signal, other_taps = from_partner((signal, taps_field), "ctx", bit_index)
        upper_half = ctx_index >> bit_index & 1 == 1
        cos_part, sin_part = unit_angles(ctx_index % half_span, 2 * half_span)
        signal = forward_section(signal, other_signal, upper_half, cos_part, sin_part)
        taps_field = forward_section(taps_field, other_taps, upper_half, cos_part, sin_part)
    return (signal, taps_field)


def butterfly_inverse(product, ctx_index, ctx_size):
    sections = ctx_size.bit_length() - 1
    for bit_index in range(sections):
        half_span = 1 << bit_index
        other_product = from_partner(product, "ctx", bit_index)
        upper_half = ctx_index >> bit_index & 1 == 1
        cos_part, sin_part = unit_angles(ctx_index % half_span, 2 * half_span)
        product = inverse_section(product, other_product, upper_half, cos_part, sin_part)
    return product


def reversed_index(ctx_index, sections):
    rank_value = jnp.zeros((), jnp.int32)
    for bit_index in range(sections):
        rank_value = rank_value + (ctx_index >> bit_index & 1) * (1 << sections - 1 - bit_index)
    return rank_value


def local_matrices(rank_value, ctx_size, local_rows):
    padded_length = 2 * ctx_size * local_rows
    freq_index = jnp.arange(local_rows, dtype=jnp.int32)[:, None]
    time_index = jnp.arange(local_rows, dtype=jnp.int32)[None, :]
    cos_list = []
    sin_list = []
    for branch_index in range(2):
        frequency = 2 * ctx_size * freq_index + 2 * rank_value + branch_index
        cos_part, sin_part = unit_angles(time_index * frequency, padded_length)
        cos_list.append(cos_part)
        sin_list.append(sin_part)
    return (jnp.stack(cos_list), jnp.stack(sin_list))


def local_forward(values_now, cos_matrix, sin_matrix):
    real_part, imag_part = (values_now[:, 0], values_now[:, 1])
    out_real = jnp.einsum("ckm,cmw->ckw", cos_matrix, real_part, precision=highest) + jnp.einsum(
        "ckm,cmw->ckw", sin_matrix, imag_part, precision=highest
    )
    out_imag = jnp.einsum("ckm,cmw->ckw", cos_matrix, imag_part, precision=highest) - jnp.einsum(
        "ckm,cmw->ckw", sin_matrix, real_part, precision=highest
    )
    return jnp.stack([out_real, out_imag], axis=1)


def local_inverse(values_now, cos_matrix, sin_matrix):
    real_part, imag_part = (values_now[:, 0], values_now[:, 1])
    out_real = jnp.einsum("ckm,ckw->cmw", cos_matrix, real_part, precision=highest) - jnp.einsum(
        "ckm,ckw->cmw", sin_matrix, imag_part, precision=highest
    )
    out_imag = jnp.einsum("ckm,ckw->cmw", cos_matrix, imag_part, precision=highest) + jnp.einsum(
        "ckm,ckw->cmw", sin_matrix, real_part, precision=highest
    )
    return jnp.stack([out_real, out_imag], axis=1)


def spectral_middle(signal, taps_field, rank_value, ctx_size):
    local_rows = signal.shape[2]
    group_size = signal.shape[3] // taps_field.shape[3]
    cos_matrix, sin_matrix = local_matrices(rank_value, ctx_size, local_rows)
    signal_spectrum = local_forward(signal, cos_matrix, sin_matrix)
    taps_spectrum = jnp.repeat(
        local_forward(taps_field, cos_matrix, sin_matrix), group_size, axis=3
    )
    product_real = (
        signal_spectrum[:, 0] * taps_spectrum[:, 0] - signal_spectrum[:, 1] * taps_spectrum[:, 1]
    )
    product_imag = (
        signal_spectrum[:, 0] * taps_spectrum[:, 1] + signal_spectrum[:, 1] * taps_spectrum[:, 0]
    )
    return local_inverse(jnp.stack([product_real, product_imag], axis=1), cos_matrix, sin_matrix)


def recombine(values_now, ctx_index, ctx_size):
    padded_length = 2 * ctx_size * values_now.shape[2]
    cos_part, sin_part = unit_angles(ctx_index, 2 * ctx_size)
    return (
        values_now[0, 0] + values_now[1, 0] * cos_part - values_now[1, 1] * sin_part
    ) / padded_length


def per_device(
    hyena_query,
    hyena_key,
    token_ids,
    embed_table,
    norm_gain,
    hyena_filter,
    attn_query,
    attn_key,
    document_ids,
):
    local_rows, local_width = hyena_query.shape
    vocab_rows = embed_table.shape[0]
    ctx_size = lax.axis_size("ctx")
    ctx_index = lax.axis_index("ctx")
    one_hot = (token_ids[:, None] == jnp.arange(vocab_rows, dtype=jnp.int32)[None, :]).astype(
        jnp.bfloat16
    )
    picked = jnp.dot(one_hot, embed_table, preferred_element_type=jnp.float32)
    square_sum = lax.psum(jnp.sum(picked * picked, axis=1), "ch")
    mean_square = square_sum / (local_width * lax.axis_size("ch"))
    normed = picked * lax.rsqrt(mean_square + epsilon)[:, None] * norm_gain
    source = hyena_key.astype(jnp.float32) * normed
    signal_start = prepare(source, ctx_index, ctx_size)
    signal, taps_field = butterfly_forward(
        signal_start, prepare(hyena_filter, ctx_index, ctx_size), ctx_index, ctx_size
    )
    rank_value = reversed_index(ctx_index, ctx_size.bit_length() - 1)
    product = spectral_middle(signal, taps_field, rank_value, ctx_size)
    inverted = butterfly_inverse(product, ctx_index, ctx_size)
    convolved = recombine(inverted, ctx_index, ctx_size)
    hyena_out = (hyena_query.astype(jnp.float32) * convolved).astype(jnp.bfloat16)
    head_count = local_width // HEAD_DIM
    score_scale = HEAD_DIM ** (-0.5)
    queries = attn_query.reshape(local_rows, head_count, HEAD_DIM)
    positions = ctx_index * local_rows + jnp.arange(local_rows, dtype=jnp.int32)
    tile_lookup_vectors = lax.all_gather(attn_key, "ctx", axis=0, tiled=True)
    block_values = lax.all_gather(hyena_out, "ctx", axis=0, tiled=True)
    block_docs = lax.all_gather(document_ids, "ctx", axis=0, tiled=True)
    block_size = tile_lookup_vectors.shape[0]
    key_positions = jnp.arange(block_size, dtype=jnp.int32)
    allowed = (key_positions[None, :] <= positions[:, None]) & (
        block_docs[None, :] == document_ids[:, None]
    )
    top_old = jnp.full((head_count, local_rows), masked_score, jnp.float32)
    scores = (
        jnp.einsum(
            "qhd,khd->hqk",
            queries,
            tile_lookup_vectors.reshape(block_size, head_count, HEAD_DIM),
            preferred_element_type=jnp.float32,
        )
        * score_scale
    )
    scores = jnp.where(allowed[None], scores, masked_score)
    top_new = jnp.maximum(top_old, jnp.max(scores, axis=2))
    weights = jnp.where(allowed[None], jnp.exp(scores - top_new[:, :, None]), 0.0)
    total_new = jnp.sum(weights, axis=2)
    numer_new = jnp.einsum(
        "hqk,khd->hqd",
        weights.astype(jnp.bfloat16),
        block_values.reshape(block_size, head_count, HEAD_DIM),
        preferred_element_type=jnp.float32,
    )
    attn_out = (
        (numer_new / total_new[:, :, None])
        .transpose(1, 0, 2)
        .reshape(local_rows, local_width)
        .astype(jnp.bfloat16)
    )
    return (hyena_out, attn_out)


def solution(mesh):
    placed = (
        P("ctx", "ch"),
        P("ctx", "ch"),
        P("ctx"),
        P(None, "ch"),
        P("ch"),
        P("ctx", "ch"),
        P("ctx", "ch"),
        P("ctx", "ch"),
        P("ctx"),
    )
    return jax.shard_map(
        per_device,
        mesh=mesh,
        in_specs=placed,
        out_specs=(P("ctx", "ch"), P("ctx", "ch")),
        check_vma=False,
    )
```

profile of v0, /device:TPU:1, one launch (start us, length us, event | category | flops | bytes accessed | tf_op | source)
XLA Modules:
  0.0 570.3 jit_solution(6359617483650990441)
XLA Ops:
  8.4 1.1 multiply_reduce_fusion
  9.5 9.3 %psum.7 = f32[128]{0:T(128)S(1)} all-reduce(f32[128]{0:T(128)S(1)} %get-tuple-element.61), channel_id=1, replica_groups=mesh['ctx'=32,'ch'=4] {'ch'}, use_global_device_ids=true, to_apply=%region_1.0 | all-reduce | flops 128 | bytes 1024 | tf_op jit(solution)/shard_map/psum | solution.py:166
  18.8 1.2 fusion.74
  20.2 1.5 pad_maximum_fusion
  21.8 2.9 collective-permute-start
  24.9 43.2 %collective-permute-done = f32[2,2,128,1024]{3,2,1,0:T(8,128)} collective-permute-done((f32[2,2,128,1024]{3,2,1,0:T(8,128)}, f32[2,2,128,1024]{3,2,1,0:T(8,128)}, u32[]{:S(2)}, u32[]{:S(2)}) %collective-permute-start) | collective-permute-done | bytes 2097184 | tf_op jit(solution)/shard_map/ppermute | solution.py:19
  68.0 2.0 fusion.75
  70.3 4.0 maximum_select_fusion
  74.4 1.3 collective-permute-start.1
  75.8 42.4 %collective-permute-done.1 = f32[2,2,128,1024]{3,2,1,0:T(8,128)} collective-permute-done((f32[2,2,128,1024]{3,2,1,0:T(8,128)}, f32[2,2,128,1024]{3,2,1,0:T(8,128)}, u32[]{:S(2)}, u32[]{:S(2)}) %collective-permute-start.1) | collective-permute-done | bytes 2097184 | tf_op jit(solution)/shard_map/ppermute | solution.py:19
  118.2 3.4 fusion.84
  122.9 4.8 maximum_select_fusion.1
  127.7 3.6 collective-permute-start.2
  131.3 3.0 collective-permute-start.5
  134.5 2.3 collective-permute-done.5
  136.7 36.1 %collective-permute-done.2 = f32[2,2,128,1024]{3,2,1,0:T(8,128)S(1)} collective-permute-done((f32[2,2,128,1024]{3,2,1,0:T(8,128)}, f32[2,2,128,1024]{3,2,1,0:T(8,128)S(1)}, u32[]{:S(2)}, u32[]{:S(2)}) %collective-permute-start.2) | collective-permute-done | bytes 2097184 | tf_op jit(solution)/shard_map/ppermute | solution.py:19
  172.9 2.7 sub.152
  175.9 2.9 maximum_select_fusion.2
  179.7 1.4 collective-permute-start.6
  181.1 2.5 collective-permute-done.6
  183.7 3.4 collective-permute-start.7
  188.2 42.8 %collective-permute-done.7 = f32[2,2,128,64]{2,3,0,1:T(8,128)S(1)} collective-permute-done((f32[2,2,128,64]{2,3,0,1:T(8,128)S(1)}, f32[2,2,128,64]{2,3,0,1:T(8,128)S(1)}, u32[]{:S(2)}, u32[]{:S(2)}) %collective-permute-start.7) | collective-permute-done | bytes 131104 | tf_op jit(solution)/shard_map/ppermute | solution.py:19
  231.5 6.8 %collective-permute-done.8 = f32[2,2,128,64]{2,3,0,1:T(8,128)S(1)} collective-permute-done((f32[2,2,128,64]{2,3,0,1:T(8,128)S(1)}, f32[2,2,128,64]{2,3,0,1:T(8,128)S(1)}, u32[]{:S(2)}, u32[]{:S(2)}) %collective-permute-start.8) | collective-permute-done | bytes 131104 | tf_op jit(solution)/shard_map/ppermute | solution.py:19
  238.3 2.0 sub.154
  240.7 3.6 maximum_select_fusion.3
  244.2 19.2 %collective-permute-start.4 = (f32[2,2,128,1024]{3,2,1,0:T(8,128)}, f32[2,2,128,1024]{3,2,1,0:T(8,128)S(1)}, u32[]{:S(2)}, u32[]{:S(2)}) collective-permute-start(f32[2,2,128,1024]{3,2,1,0:T(8,128)} %maximum_select_fusion.3), channel_id=1, source_target_pairs={{0,4},{4,0},{8,12},{12,8},{16,20},{20,16},{24,28},{28,24},{32,36},... | collective-permute-start | bytes 6291464 | tf_op jit(solution)/shard_map/ppermute | solution.py:19
  264.4 3.0 collective-permute-done.9
  269.2 1.2 fusion.76
  270.4 2.5 copy.58
  272.9 1.4 copy.59
  274.3 2.0 sub.156
  276.5 2.3 maximum_select_fusion.4
  282.3 1.3 fusion.17
  286.8 1.1 convolution_add_fusion
  289.2 3.5 collective-permute-done.10
  294.6 46.5 %collective-permute-done.11 = f32[2,2,128,1024]{3,2,1,0:T(8,128)S(1)} collective-permute-done((f32[2,2,128,1024]{3,2,1,0:T(8,128)S(1)}, f32[2,2,128,1024]{3,2,1,0:T(8,128)S(1)}, u32[]{:S(2)}, u32[]{:S(2)}) %collective-permute-start.11) | collective-permute-done | bytes 2097184 | tf_op jit(solution)/shard_map/ppermute | solution.py:19
  343.1 47.0 %collective-permute-done.12 = f32[2,2,128,1024]{3,2,1,0:T(8,128)S(1)} collective-permute-done((f32[2,2,128,1024]{3,2,1,0:T(8,128)S(1)}, f32[2,2,128,1024]{3,2,1,0:T(8,128)S(1)}, u32[]{:S(2)}, u32[]{:S(2)}) %collective-permute-start.12) | collective-permute-done | bytes 2097184 | tf_op jit(solution)/shard_map/ppermute | solution.py:19
  391.6 1.4 collective-permute-start.13
  393.3 43.4 %collective-permute-done.13 = f32[2,2,128,1024]{3,2,1,0:T(8,128)S(1)} collective-permute-done((f32[2,2,128,1024]{3,2,1,0:T(8,128)S(1)}, f32[2,2,128,1024]{3,2,1,0:T(8,128)S(1)}, u32[]{:S(2)}, u32[]{:S(2)}) %collective-permute-start.13) | collective-permute-done | bytes 2097184 | tf_op jit(solution)/shard_map/ppermute | solution.py:19
  438.1 2.9 collective-permute-start.14
  441.3 42.5 %collective-permute-done.14 = f32[2,2,128,1024]{3,2,1,0:T(8,128)S(1)} collective-permute-done((f32[2,2,128,1024]{3,2,1,0:T(8,128)S(1)}, f32[2,2,128,1024]{3,2,1,0:T(8,128)S(1)}, u32[]{:S(2)}, u32[]{:S(2)}) %collective-permute-start.14) | collective-permute-done | bytes 2097184 | tf_op jit(solution)/shard_map/ppermute | solution.py:19
  486.3 24.9 %all-gather = s32[32,1,128]{2,1,0:T(1,128)S(1)} all-gather(s32[1,1,128]{2,1,0:T(1,128)S(1)} %bitcast.109), channel_id=1, replica_groups=mesh['ctx'=32,'ch'=4] {'ctx'}, dimensions={0}, use_global_device_ids=true | all-gather | bytes 16896 | tf_op jit(solution)/shard_map/all_gather | solution.py:185
  511.7 6.3 %fusion = (f32[8,128]{1,0:T(8,128)S(1)}, f32[8,128,4096]{2,1,0:T(8,128)S(1)}) fusion(pred[128,4096]{1,0:T(8,128)(4,1)S(1)} %fusion.11, bf16[4096,8,128]{0,2,1:T(8,128)(2,1)} %bitcast.102, bf16[128,1024]{1,0:T(8,128)(2,1)S(1)} %copy-done.8), kind=kOutput, calls=%fused_computation.2 | convolution fusion | flops 1086323712 | bytes 25956352 | tf_op jit(solution)/shard_map/qhd,khd->hqk/dot_general | solution.py:193
  518.0 5.8 %copy-done.2 = f32[8,128,4096]{2,1,0:T(8,128)} copy-done((f32[8,128,4096]{2,1,0:T(8,128)}, f32[8,128,4096]{2,1,0:T(8,128)S(1)}, u32[]{:S(2)}) %copy-start.2) | copy-done | bytes 16777240
  523.8 5.4 fusion.1
  529.2 10.7 %all-gather.6.cloned.1.call-done = bf16[4096,1024]{1,0:T(8,128)(2,1)} async-done(((bf16[128,1024]{1,0:T(8,128)(2,1)}), bf16[4096,1024]{1,0:T(8,128)(2,1)}) %all-gather.6.cloned.1.call-update) | async-done | bytes 8388624 | tf_op jit(solution)/shard_map/all_gather | solution.py:184
  539.8 11.6 %copy.57 = bf16[4096,1024]{0,1:T(8,128)(2,1)} copy(bf16[4096,1024]{1,0:T(8,128)(2,1)} %all-gather.6.cloned.1.call-done) | data formatting | bytes 16777216 | tf_op jit(solution)/shard_map/reshape | solution.py:208
  551.5 10.9 %fusion.22 = bf16[128,8,128]{0,2,1:T(8,128)(2,1)S(1)} fusion(bf16[4096,8,128]{0,2,1:T(8,128)(2,1)} %bitcast.103, f32[8,128,4096]{2,1,0:T(8,128)} %copy-done.2, f32[8,128]{1,0:T(8,128)S(1)} %broadcast_maximum_fusion, pred[128,4096]{1,0:T(8,128)(4,1)S(1)} %fusion.11, f32[128,8]{0,1:T(8,128)S(1)} %bitcast.108), kind=kOutput, calls=%fused_computation.81 | convolution fusion | flops 1094975488 | bytes 25960448 | tf_op jit(solution)/shard_map/hqk,khd->hqd/dot_general | solution.py:205
  (102 shorter events, 27.7 us)
Async XLA Ops:
  7.2 1.2 copy-start
  7.2 504.5 %all-gather.4.cloned.1.call-start = ((), (), s32[]{:S(2)}) async-start(), calls=%async_computation | async-start | bytes 8650752 | tf_op jit(solution)/shard_map/all_gather | solution.py:183
  21.8 46.2 %collective-permute-start = (f32[2,2,128,1024]{3,2,1,0:T(8,128)}, f32[2,2,128,1024]{3,2,1,0:T(8,128)}, u32[]{:S(2)}, u32[]{:S(2)}) collective-permute-start(f32[2,2,128,1024]{3,2,1,0:T(8,128)} %pad_maximum_fusion), channel_id=1, source_target_pairs={{0,64},{4,68},{8,72},{12,76},{16,80},{20,84},{24,88},{28,92},{32,9... | collective-permute-start | bytes 6291464 | tf_op jit(solution)/shard_map/ppermute | solution.py:19
  70.3 4.0 copy-start.3
  74.4 43.8 %collective-permute-start.1 = (f32[2,2,128,1024]{3,2,1,0:T(8,128)}, f32[2,2,128,1024]{3,2,1,0:T(8,128)}, u32[]{:S(2)}, u32[]{:S(2)}) collective-permute-start(f32[2,2,128,1024]{3,2,1,0:T(8,128)} %maximum_select_fusion), channel_id=1, source_target_pairs={{0,32},{4,36},{8,40},{12,44},{16,48},{20,52},{24,56},{28,60},{32,0... | collective-permute-start | bytes 6291464 | tf_op jit(solution)/shard_map/ppermute | solution.py:19
  121.6 1.2 copy-start.4
  122.8 8.4 %copy-start.11 = (f32[128,64]{0,1:T(8,128)S(1)}, f32[128,64]{0,1:T(8,128)}, u32[]{:S(2)}) copy-start(f32[128,64]{0,1:T(8,128)} %param.14) | copy-start | bytes 98308
  127.7 45.2 %collective-permute-start.2 = (f32[2,2,128,1024]{3,2,1,0:T(8,128)}, f32[2,2,128,1024]{3,2,1,0:T(8,128)S(1)}, u32[]{:S(2)}, u32[]{:S(2)}) collective-permute-start(f32[2,2,128,1024]{3,2,1,0:T(8,128)} %maximum_select_fusion.1), channel_id=1, source_target_pairs={{0,16},{4,20},{8,24},{12,28},{16,0},{20,4},{24,8},{28,12},{32,48},... | collective-permute-start | bytes 6291464 | tf_op jit(solution)/shard_map/ppermute | solution.py:19
  131.3 5.4 collective-permute-start.5
  172.9 2.7 copy-start.5
  178.8 8.3 %copy-start.9 = (bf16[128,1024]{1,0:T(8,128)(2,1)S(1)}, bf16[128,1024]{1,0:T(8,128)(2,1)}, u32[]{:S(2)}) copy-start(bf16[128,1024]{1,0:T(8,128)(2,1)} %param.16) | copy-start | bytes 786436
  178.8 59.5 %collective-permute-start.3 = (f32[2,2,128,1024]{3,2,1,0:T(8,128)S(1)}, f32[2,2,128,1024]{3,2,1,0:T(8,128)}, u32[]{:S(2)}, u32[]{:S(2)}) collective-permute-start(f32[2,2,128,1024]{3,2,1,0:T(8,128)S(1)} %maximum_select_fusion.2), channel_id=1, source_target_pairs={{0,8},{4,12},{8,0},{12,4},{16,24},{20,28},{24,16},{28,20},{32,40},... | collective-permute-start | bytes 6291464 | tf_op jit(solution)/shard_map/ppermute | solution.py:19
  179.7 3.9 collective-permute-start.6
  183.7 47.3 %collective-permute-start.7 = (f32[2,2,128,64]{2,3,0,1:T(8,128)S(1)}, f32[2,2,128,64]{2,3,0,1:T(8,128)S(1)}, u32[]{:S(2)}, u32[]{:S(2)}) collective-permute-start(f32[2,2,128,64]{2,3,0,1:T(8,128)S(1)} %maximum_select_fusion.6), channel_id=1, source_target_pairs={{0,16},{4,20},{8,24},{12,28},{16,0},{20,4},{24,8},{28,12},{32,48},... | collective-permute-start | bytes 393224 | tf_op jit(solution)/shard_map/ppermute | solution.py:19
  188.0 351.9 %all-gather.6.cloned.1.call-start = ((), (), s32[]{:S(2)}) async-start(), calls=%async_computation.1 | async-start | bytes 8650752 | tf_op jit(solution)/shard_map/all_gather | solution.py:184
  231.1 7.2 %collective-permute-start.8 = (f32[2,2,128,64]{2,3,0,1:T(8,128)S(1)}, f32[2,2,128,64]{2,3,0,1:T(8,128)S(1)}, u32[]{:S(2)}, u32[]{:S(2)}) collective-permute-start(f32[2,2,128,64]{2,3,0,1:T(8,128)S(1)} %maximum_select_fusion.7), channel_id=1, source_target_pairs={{0,8},{4,12},{8,0},{12,4},{16,24},{20,28},{24,16},{28,20},{32,40},... | collective-permute-start | bytes 393224 | tf_op jit(solution)/shard_map/ppermute | solution.py:19
  244.2 30.0 %collective-permute-start.4 = (f32[2,2,128,1024]{3,2,1,0:T(8,128)}, f32[2,2,128,1024]{3,2,1,0:T(8,128)S(1)}, u32[]{:S(2)}, u32[]{:S(2)}) collective-permute-start(f32[2,2,128,1024]{3,2,1,0:T(8,128)} %maximum_select_fusion.3), channel_id=1, source_target_pairs={{0,4},{4,0},{8,12},{12,8},{16,20},{20,16},{24,28},{28,24},{32,36},... | collective-permute-start | bytes 6291464 | tf_op jit(solution)/shard_map/ppermute | solution.py:19
  263.5 3.9 collective-permute-start.9
  280.8 1.2 copy-start.6
  280.8 1.5 copy-start.7
  288.3 4.4 collective-permute-start.10
  294.2 46.9 %collective-permute-start.11 = (f32[2,2,128,1024]{3,2,1,0:T(8,128)S(1)}, f32[2,2,128,1024]{3,2,1,0:T(8,128)S(1)}, u32[]{:S(2)}, u32[]{:S(2)}) collective-permute-start(f32[2,2,128,1024]{3,2,1,0:T(8,128)S(1)} %fusion.6), channel_id=1, source_target_pairs={{0,8},{4,12},{8,0},{12,4},{16,24},{20,28},{24,16},{28,20},{32,40},... | collective-permute-start | bytes 6291464 | tf_op jit(solution)/shard_map/ppermute | solution.py:19
  342.6 47.5 %collective-permute-start.12 = (f32[2,2,128,1024]{3,2,1,0:T(8,128)S(1)}, f32[2,2,128,1024]{3,2,1,0:T(8,128)S(1)}, u32[]{:S(2)}, u32[]{:S(2)}) collective-permute-start(f32[2,2,128,1024]{3,2,1,0:T(8,128)S(1)} %fusion.7), channel_id=1, source_target_pairs={{0,16},{4,20},{8,24},{12,28},{16,0},{20,4},{24,8},{28,12},{32,48},... | collective-permute-start | bytes 6291464 | tf_op jit(solution)/shard_map/ppermute | solution.py:19
  391.6 45.1 %collective-permute-start.13 = (f32[2,2,128,1024]{3,2,1,0:T(8,128)S(1)}, f32[2,2,128,1024]{3,2,1,0:T(8,128)S(1)}, u32[]{:S(2)}, u32[]{:S(2)}) collective-permute-start(f32[2,2,128,1024]{3,2,1,0:T(8,128)S(1)} %fusion.8), channel_id=1, source_target_pairs={{0,32},{4,36},{8,40},{12,44},{16,48},{20,52},{24,56},{28,60},{32,0... | collective-permute-start | bytes 6291464 | tf_op jit(solution)/shard_map/ppermute | solution.py:19
  438.1 45.7 %collective-permute-start.14 = (f32[2,2,128,1024]{3,2,1,0:T(8,128)S(1)}, f32[2,2,128,1024]{3,2,1,0:T(8,128)S(1)}, u32[]{:S(2)}, u32[]{:S(2)}) collective-permute-start(f32[2,2,128,1024]{3,2,1,0:T(8,128)S(1)} %fusion.9), channel_id=1, source_target_pairs={{0,64},{4,68},{8,72},{12,76},{16,80},{20,84},{24,88},{28,92},{32,9... | collective-permute-start | bytes 6291464 | tf_op jit(solution)/shard_map/ppermute | solution.py:19
  484.2 1.1 copy-start.10
  485.3 0.9 copy-start.12
  485.3 26.3 %copy-start.8 = (bf16[128,1024]{1,0:T(8,128)(2,1)S(1)}, bf16[128,1024]{1,0:T(8,128)(2,1)}, u32[]{:S(2)}) copy-start(bf16[128,1024]{1,0:T(8,128)(2,1)} %param.15) | copy-start | bytes 786436
  518.0 5.8 %copy-start.2 = (f32[8,128,4096]{2,1,0:T(8,128)}, f32[8,128,4096]{2,1,0:T(8,128)S(1)}, u32[]{:S(2)}) copy-start(f32[8,128,4096]{2,1,0:T(8,128)S(1)} %get-tuple-element.64) | copy-start | bytes 50331652
  551.5 11.7 %copy-start.1 = (bf16[512,1024]{1,0:T(8,128)(2,1)S(1)}, bf16[512,1024]{1,0:T(8,128)(2,1)}, u32[]{:S(2)}) copy-start(bf16[512,1024]{1,0:T(8,128)(2,1)} %param.12) | copy-start | bytes 3145732
Sparse Core Ops, SparseCore 0:
  188.1 71.1 all-gather.3
  486.4 53.4 all-gather.5
where the time goes:
time: 579 us; the launch traced here: 570 us
  waiting for transfers between devices  373 us (64%)
  other arithmetic  51.1 us (9%)
  starting transfers between devices  41.4 us (7%)
  blocking collectives  34.2 us (6%)
  matrix products  28.4 us (5%)
  local copies, waits for them, and re-layouts  26.9 us (5%)
  between operations  15.8 us (3%)
    ppermute x15, waiting for transfers between devices, from_partner(): return lax.ppermute(value, axis, pairs)  362 us
    ppermute x15, starting transfers between devices, from_partner(): return lax.ppermute(value, axis, pairs)  41.3 us
    all_gather x1, blocking collectives, per_device(): block_docs = lax.all_gather(document_ids, 'ctx', axis=0, tiled=True)  24.9 us
    select_n x10, other arithmetic, forward_section(): return jnp.where(upper_half, upper_result, lower_result)  17.7 us
    unnamed x30, local copies, waits for them, and re-layouts  13.8 us
    sub x10, other arithmetic, forward_section(): upper_result = rotate(other_values - own_values, cos_part, -sin_part)  12.3 us
    reshape x1, local copies, waits for them, and re-layouts, per_device(): block_values.reshape(block_size, head_count, HEAD_DIM)  11.6 us
  transfers between devices with their start and end apart: 17, of which 14 were waited for; matrix products, arithmetic and copies ran while one was open for 9% of the time, Pallas kernels for 0%

commit v1 on v0

v1 whole, which is shorter than its diff:
```python
import functools
import math

import jax
import jax.numpy as jnp
from jax import lax
from jax.experimental import pallas as pl
from jax.experimental.pallas import tpu as pltpu
from jax.sharding import PartitionSpec as P

MESH = pl.DeviceIdType.MESH
F32 = jnp.float32
BF16 = jnp.bfloat16

CTX = 32
CH = 4
ROWS = 128
WIDTH = 1024
VOCAB = 512
CHANNELS = 4096
OWN = 32
GROUP = 16
HEAD_DIM = 128
PAD = 2048
WINDOW = PAD + ROWS
EPSILON = 1e-06
MASKED = -1e30
EXPONENT = HEAD_DIM**-0.5 * math.log2(math.e)

META, SOURCE, GATE, QUERY, KEY, KEY_PAIR, VALUE_PAIR, HOME, ATTN, SQUARES = range(10)


def nt_dot(a, b):
    return lax.dot_general(a, b, (((1,), (1,)), ((), ())), preferred_element_type=F32)


def nn_dot(a, b):
    return jnp.dot(a, b, preferred_element_type=F32)


def halves(value):
    high = value.astype(BF16)
    return high, (value - high.astype(F32)).astype(BF16)


def kernel(
    ids_ref,
    docs_ref,
    table_ref,
    gain_ref,
    gate_ref,
    key_ref,
    filter_ref,
    attn_query_ref,
    attn_key_ref,
    hyena_out_ref,
    attn_out_ref,
    squares,
    meta_out,
    meta_in,
    source_out,
    source_in,
    gate_out,
    gate_in,
    toeplitz,
    sums,
    values_t,
    values,
    keys,
    queries,
    docs_row,
    home_in,
    attn_t,
    attn_in,
    send,
    recv,
    local,
):
    me = lax.axis_index("ctx")
    my_ch = lax.axis_index("ch")
    core = lax.rem(me, 2)
    mine = lax.div(me, 2)
    pair = me + 1 - 2 * core

    def remote(src, dst, kind, to):
        return pltpu.make_async_remote_copy(
            src_ref=src,
            dst_ref=dst,
            send_sem=send.at[kind],
            recv_sem=recv.at[kind],
            device_id=to,
            device_id_type=MESH,
        )

    def wait_in(ref, kind):
        pltpu.make_async_copy(ref, ref, recv.at[kind]).wait()

    def wait_out(ref, kind):
        pltpu.make_async_copy(ref, ref, send.at[kind]).wait()

    barrier = pltpu.get_barrier_semaphore()

    @pl.loop(1, CTX)
    def _(r):
        pl.semaphore_signal(
            barrier, inc=1, device_id={"ctx": lax.rem(me + r, CTX)}, device_id_type=MESH
        )

    for r in range(1, CH):
        pl.semaphore_signal(
            barrier, inc=1, device_id={"ch": lax.rem(my_ch + r, CH)}, device_id_type=MESH
        )

    by_lane = jnp.zeros((VOCAB, 128), F32)
    for tile in range(WIDTH // 128):
        part = table_ref[:, tile * 128 : (tile + 1) * 128].astype(F32)
        by_lane = by_lane + part * part
    high, low = halves(by_lane)
    ones = jnp.ones((8, 128), BF16)
    squares[my_ch] = nt_dot(ones, high) + nt_dot(ones, low)

    taps = jnp.concatenate([filter_ref[...], jnp.zeros((ROWS, 64), F32)], axis=1).T
    docs = docs_ref[...].astype(F32)
    for d in range(CTX):
        meta_out[d] = jnp.concatenate([taps[2 * d : 2 * d + 2], docs, docs], axis=0)
    meta_in[me] = meta_out[me]

    pl.semaphore_wait(barrier, CTX - 1 + CH - 1)

    for r in range(1, CH):
        to = lax.rem(my_ch + r, CH)
        remote(squares.at[my_ch], squares.at[my_ch], SQUARES, {"ch": to}).start()

    @pl.loop(1, CTX)
    def _(r):
        to = lax.rem(me + r, CTX)
        remote(meta_out.at[to], meta_in.at[me], META, {"ctx": to}).start()

    one_hot_t = (lax.broadcasted_iota(jnp.int32, (VOCAB, ROWS), 0) == ids_ref[...]).astype(F32)
    picked = nn_dot(one_hot_t.T.astype(BF16), table_ref[...])
    product_t = (picked * key_ref[...].astype(F32) * gain_ref[...]).T

    wait_in(squares.at[pl.ds(0, CH - 1)], SQUARES)
    total = squares[0] + squares[1] + squares[2] + squares[3]
    high, low = halves(total)
    one_hot_t = one_hot_t.astype(BF16)
    mean_square = (nn_dot(high, one_hot_t) + nn_dot(low, one_hot_t)) * (1.0 / CHANNELS)
    scale = lax.rsqrt(mean_square + EPSILON)[0:1]
    source_out[...] = (product_t * scale).astype(BF16).reshape(CTX, OWN, ROWS)
    source_in[me] = source_out[me]

    @pl.loop(1, CTX)
    def _(r):
        to = lax.rem(me + r, CTX)
        remote(source_out.at[to], source_in.at[me], SOURCE, {"ctx": to}).start()

    gate_out[...] = gate_ref[...].astype(F32).T.astype(BF16).reshape(CTX, OWN, ROWS)
    gate_in[me] = gate_out[me]

    @pl.loop(1, CTX)
    def _(r):
        to = lax.rem(me + r, CTX)
        remote(gate_out.at[to], gate_in.at[me], GATE, {"ctx": to}).start()

    my_keys = keys.at[pl.ds(PAD + me * ROWS, ROWS)]
    my_head = pl.ds(pl.multiple_of(lax.div(me, 4) * HEAD_DIM, HEAD_DIM), HEAD_DIM)
    own_key = pltpu.make_async_copy(attn_key_ref.at[:, my_head], my_keys, local.at[0])
    own_query = pltpu.make_async_copy(attn_query_ref.at[:, my_head], queries.at[mine], local.at[1])
    own_key.start()
    own_query.start()

    @pl.loop(1, CTX // 2)
    def _(r):
        to = lax.rem(me + 2 * r, CTX)
        head = pl.ds(pl.multiple_of(lax.div(to, 4) * HEAD_DIM, HEAD_DIM), HEAD_DIM)
        remote(attn_key_ref.at[:, head], my_keys, KEY, {"ctx": to}).start()

    @pl.loop(1, CTX // 2)
    def _(r):
        to = lax.rem(me + 2 * r, CTX)
        head = pl.ds(pl.multiple_of(lax.div(to, 4) * HEAD_DIM, HEAD_DIM), HEAD_DIM)
        remote(attn_query_ref.at[:, head], queries.at[mine], QUERY, {"ctx": to}).start()

    wait_in(meta_in.at[pl.ds(0, CTX - 1)], META)
    down = lax.broadcasted_iota(jnp.int32, (ROWS, ROWS), 0)
    right = lax.broadcasted_iota(jnp.int32, (ROWS, ROWS), 1)
    upper = right >= down

    def turned(n, g):
        row = jnp.broadcast_to(meta_in[n, g : g + 1, :], (ROWS, ROWS))
        return pltpu.roll(row, 0, 1, stride=1, stride_axis=0)

    for g in range(2):

        def build(k, carry):
            before, block_before = carry
            first = turned(2 * k, g)
            second = turned(2 * k + 1, g)
            block = jnp.where(upper, first, before).astype(BF16)
            block_next = jnp.where(upper, second, first).astype(BF16)
            toeplitz[g, k, 0:128, 0:128] = block
            toeplitz[g, k, 128:256, 128:256] = block
            toeplitz[g, k, 0:128, 128:256] = block_next
            toeplitz[g, k, 128:256, 0:128] = block_before
            return second, block_next

        lax.fori_loop(
            0, 16, build, (jnp.zeros((ROWS, ROWS), F32), jnp.zeros((ROWS, ROWS), BF16))
        )

    docs_row[:, 0:PAD] = jnp.full((8, PAD), -1.0, F32)
    for j in range(CTX):
        docs_row[:, PAD + j * ROWS : PAD + (j + 1) * ROWS] = jnp.broadcast_to(
            meta_in[j, 2:3, :], (8, ROWS)
        )
    values[0:PAD] = jnp.zeros((PAD, 128), BF16)
    keys[0:PAD] = jnp.zeros((PAD, 128), BF16)

    wait_in(source_in.at[pl.ds(0, CTX - 1)], SOURCE)
    for g in range(2):
        own = slice(g * GROUP, (g + 1) * GROUP)
        signal = source_in[:, own, :].reshape(16, 2, GROUP, ROWS)
        signal = jnp.concatenate(
            [signal[:, half].reshape(256, ROWS) for half in range(2)], axis=1
        )
        sums[g] = nn_dot(signal, toeplitz[g, 0])
        for k in range(1, 16):
            sums[g, 16 * k :] += nn_dot(signal[: 256 - 16 * k], toeplitz[g, k])

    wait_in(gate_in.at[pl.ds(0, CTX - 1)], GATE)
    for g in range(2):
        own = slice(g * GROUP, (g + 1) * GROUP)
        convolved = jnp.stack(
            [sums[g, :, half * ROWS : (half + 1) * ROWS].reshape(16, GROUP, ROWS) for half in range(2)],
            axis=1,
        ).reshape(CTX, GROUP, ROWS)
        values_t[core, :, own, :] = (convolved * gate_in[:, own, :].astype(F32)).astype(BF16)

    remote(values_t.at[core], values_t.at[core], VALUE_PAIR, {"ctx": pair}).start()

    own_key.wait()
    own_query.wait()
    wait_in(keys.at[pl.ds(0, 15 * ROWS)], KEY)

    @pl.loop(0, 16)
    def _(q):
        block = keys.at[pl.ds(PAD + (2 * q + core) * ROWS, ROWS)]
        remote(block, block, KEY_PAIR, {"ctx": pair}).start()

    @pl.loop(1, CTX)
    def _(r):
        to = lax.rem(me + r, CTX)
        block = values_t.at[core, to]
        remote(block, home_in.at[me], HOME, {"ctx": to}).start()

    home_in[me] = values_t[core, me]

    wait_in(queries.at[pl.ds(0, 15)], QUERY)
    wait_in(values_t.at[0], VALUE_PAIR)

    @pl.loop(0, CTX)
    def _(j):
        block = jnp.concatenate(
            [
                values_t[0, j].astype(F32),
                values_t[1, j].astype(F32),
                jnp.ones((64, ROWS), F32),
            ],
            axis=0,
        )
        values[pl.ds(pl.multiple_of(PAD + j * ROWS, ROWS), ROWS)] = block.T.astype(BF16)

    wait_in(keys.at[pl.ds(0, 16 * ROWS)], KEY_PAIR)

    @pl.loop(0, 16)
    def _(q):
        block = 2 * q + core
        start = pl.multiple_of(block * ROWS, ROWS)
        window = pl.ds(start, WINDOW)
        scores = nt_dot(queries[q], keys[window])
        own_docs = docs_row[0:1, pl.ds(pl.multiple_of(PAD + start, ROWS), ROWS)]
        own_docs = jnp.broadcast_to(own_docs, (ROWS, ROWS)).T[:, 0:1]
        allowed = docs_row[0:1, window] == own_docs
        causal = lax.broadcasted_iota(jnp.int32, (ROWS, WINDOW), 1) <= PAD + (
            lax.broadcasted_iota(jnp.int32, (ROWS, WINDOW), 0)
        )
        scores = jnp.where(allowed & causal, scores, MASKED)
        top = jnp.max(scores, axis=1, keepdims=True)
        weights = jnp.exp2((scores - top) * EXPONENT).astype(BF16)
        numerator = nn_dot(weights, values[window])
        result = numerator * (1.0 / numerator[:, 64:65])
        attn_t[q] = result.T[0:64].astype(BF16)

        @pl.when(block != me)
        def _():
            remote(attn_t.at[q], attn_in.at[mine], ATTN, {"ctx": block}).start()

        @pl.when(block == me)
        def _():
            attn_in[mine] = attn_t[q]

    wait_in(home_in.at[pl.ds(0, CTX - 1)], HOME)
    hyena_out_ref[...] = home_in[...].reshape(WIDTH, ROWS).astype(F32).T.astype(BF16)
    wait_in(attn_in.at[pl.ds(0, 15)], ATTN)
    attn_out_ref[...] = attn_in[...].reshape(WIDTH, ROWS).astype(F32).T.astype(BF16)

    wait_out(squares.at[pl.ds(0, CH - 1)], SQUARES)
    wait_out(meta_in.at[pl.ds(0, CTX - 1)], META)
    wait_out(source_out.at[pl.ds(0, CTX - 1)], SOURCE)
    wait_out(gate_out.at[pl.ds(0, CTX - 1)], GATE)
    wait_out(queries.at[pl.ds(0, 15)], QUERY)
    wait_out(keys.at[pl.ds(0, 15 * ROWS)], KEY)
    wait_out(keys.at[pl.ds(0, 16 * ROWS)], KEY_PAIR)
    wait_out(values_t.at[0], VALUE_PAIR)
    wait_out(home_in.at[pl.ds(0, CTX - 1)], HOME)
    wait_out(attn_in.at[pl.ds(0, 15)], ATTN)


def per_device(
    hyena_query,
    hyena_key,
    token_ids,
    embed_table,
    norm_gain,
    hyena_filter,
    attn_query,
    attn_key,
    document_ids,
):
    vmem = pl.BlockSpec(memory_space=pltpu.VMEM)
    hbm = pl.BlockSpec(memory_space=pl.ANY)
    shape = jax.ShapeDtypeStruct((ROWS, WIDTH), BF16)
    return pl.pallas_call(
        kernel,
        out_shape=(shape, shape),
        in_specs=[vmem] * 7 + [hbm] * 2,
        out_specs=(vmem, vmem),
        scratch_shapes=[
            pltpu.VMEM((CH, 8, VOCAB), F32),
            pltpu.VMEM((CTX, 4, ROWS), F32),
            pltpu.VMEM((CTX, 4, ROWS), F32),
            pltpu.VMEM((CTX, OWN, ROWS), BF16),
            pltpu.VMEM((CTX, OWN, ROWS), BF16),
            pltpu.VMEM((CTX, OWN, ROWS), BF16),
            pltpu.VMEM((CTX, OWN, ROWS), BF16),
            pltpu.VMEM((2, 16, 256, 256), BF16),
            pltpu.VMEM((2, 256, 256), F32),
            pltpu.VMEM((2, CTX, OWN, ROWS), BF16),
            pltpu.VMEM((PAD + CTX * ROWS, 128), BF16),
            pltpu.VMEM((PAD + CTX * ROWS, 128), BF16),
            pltpu.VMEM((16, ROWS, HEAD_DIM), BF16),
            pltpu.VMEM((8, PAD + CTX * ROWS), F32),
            pltpu.VMEM((CTX, OWN, ROWS), BF16),
            pltpu.VMEM((16, 64, ROWS), BF16),
            pltpu.VMEM((16, 64, ROWS), BF16),
            pltpu.SemaphoreType.DMA((10,)),
            pltpu.SemaphoreType.DMA((10,)),
            pltpu.SemaphoreType.DMA((2,)),
        ],
        compiler_params=pltpu.CompilerParams(
            collective_id=0, has_side_effects=True, vmem_limit_bytes=48 * 1024 * 1024
        ),
    )(
        token_ids.reshape(1, ROWS),
        document_ids.reshape(1, ROWS),
        embed_table,
        norm_gain.reshape(1, WIDTH),
        hyena_query,
        hyena_key,
        hyena_filter,
        attn_query,
        attn_key,
    )


def solution(mesh):
    placed = (
        P("ctx", "ch"),
        P("ctx", "ch"),
        P("ctx"),
        P(None, "ch"),
        P("ch"),
        P("ctx", "ch"),
        P("ctx", "ch"),
        P("ctx", "ch"),
        P("ctx"),
    )
    return jax.shard_map(
        per_device,
        mesh=mesh,
        in_specs=placed,
        out_specs=(P("ctx", "ch"), P("ctx", "ch")),
        check_vma=False,
    )
```

time: 579 us -> 60 us (0.10)
  the two profiles are of different devices: /device:TPU:1 before, /device:TPU:24 now
where the time goes in v1:
time: 60 us; the launch traced here: 59.6 us
  Pallas kernels  51.6 us (86%)
  local copies, waits for them, and re-layouts  7.3 us (12%)
  between operations  0.7 us (1%)
    pallas_call x1, Pallas kernels, per_device(): pl.pallas_call(kernel, out_shape=(shape, shape), in_specs=[vmem] * 7 + [h...  51.6 us
    unnamed x19, local copies, waits for them, and re-layouts  7.3 us

profile of v1, /device:TPU:24, one launch (start us, length us, event | category | flops | bytes accessed | tf_op | source)
XLA Modules:
  0.0 59.6 jit_solution(1494430608459259159)
XLA Ops:
  0.6 0.0 copy-start.5
  0.6 0.0 copy-start.6
  0.7 0.0 copy-start.7
  0.7 0.9 %copy.11.filter_ref = f32[128,64]{1,0:T(8,128)S(1)} copy(f32[128,64]{0,1:T(8,128)} %param.14) | data formatting | bytes 65536 | tf_op args[5]
  1.5 0.0 copy-done.5
  1.5 0.0 copy-done.6
  1.6 0.0 copy-done.7
  1.6 0.0 copy-start
  1.6 1.2 %copy-done = bf16[512,1024]{1,0:T(8,128)(2,1)S(1)} copy-done((bf16[512,1024]{1,0:T(8,128)(2,1)S(1)}, bf16[512,1024]{1,0:T(8,128)(2,1)}, u32[]{:S(2)}) %copy-start) | copy-done | bytes 1048600
  2.8 0.0 copy-start.1
  2.8 0.9 %copy-done.1 = bf16[128,1024]{1,0:T(8,128)(2,1)S(1)} copy-done((bf16[128,1024]{1,0:T(8,128)(2,1)S(1)}, bf16[128,1024]{1,0:T(8,128)(2,1)}, u32[]{:S(2)}) %copy-start.1) | copy-done | bytes 262168
  3.7 0.0 copy-start.2
  3.7 0.9 %copy-done.2 = bf16[128,1024]{1,0:T(8,128)(2,1)S(1)} copy-done((bf16[128,1024]{1,0:T(8,128)(2,1)S(1)}, bf16[128,1024]{1,0:T(8,128)(2,1)}, u32[]{:S(2)}) %copy-start.2) | copy-done | bytes 262168
  4.7 0.0 copy-start.3
  4.7 0.9 %copy-done.3 = bf16[128,1024]{1,0:T(8,128)(2,1)S(1)} copy-done((bf16[128,1024]{1,0:T(8,128)(2,1)S(1)}, bf16[128,1024]{1,0:T(8,128)(2,1)}, u32[]{:S(2)}) %copy-start.3) | copy-done | bytes 262168
  5.6 0.0 copy-start.4
  5.6 0.9 %copy-done.4 = bf16[128,1024]{1,0:T(8,128)(2,1)S(1)} copy-done((bf16[128,1024]{1,0:T(8,128)(2,1)S(1)}, bf16[128,1024]{1,0:T(8,128)(2,1)}, u32[]{:S(2)}) %copy-start.4) | copy-done | bytes 262168
  6.6 51.6 %shard_map.104 = (bf16[128,1024]{1,0:T(8,128)(2,1)S(1)}, bf16[128,1024]{1,0:T(8,128)(2,1)S(1)}) custom-call(s32[1,128]{1,0:T(1,128)S(1)} %bitcast.4, s32[1,128]{1,0:T(1,128)S(1)} %bitcast.5, bf16[512,1024]{1,0:T(8,128)(2,1)S(1)} %copy-done, f32[1,1024]{1,0:T(1,128)S(1)} %bitcast.3, bf16[128,1024]{1,0:T(8,128)(2,1)S(1)} %copy-done.1, ...), custom_call_target="tpu_custom_call" | custom-call | tf_op jit(solution)/shard_map/pallas_call | solution.py:333
  58.2 0.7 %copy.14 = bf16[128,1024]{1,0:T(8,128)(2,1)} copy(bf16[128,1024]{1,0:T(8,128)(2,1)S(1)} %get-tuple-element.4) | data formatting | bytes 524288
  58.9 0.7 %copy.15 = bf16[128,1024]{1,0:T(8,128)(2,1)} copy(bf16[128,1024]{1,0:T(8,128)(2,1)S(1)} %get-tuple-element.5) | data formatting | bytes 524288
Async XLA Ops:
  0.6 0.9 %copy-start.5 = (f32[1024]{0:T(1024)S(1)}, f32[1024]{0:T(1024)}, u32[]{:S(2)}) copy-start(f32[1024]{0:T(1024)} %param.13) | copy-start | bytes 12292
  0.6 0.9 %copy-start.6 = (s32[128]{0:T(128)S(1)}, s32[128]{0:T(128)}, u32[]{:S(2)}) copy-start(s32[128]{0:T(128)} %param.11) | copy-start | bytes 1540
  0.7 0.9 %copy-start.7 = (s32[128]{0:T(128)S(1)}, s32[128]{0:T(128)}, u32[]{:S(2)}) copy-start(s32[128]{0:T(128)} %param.17) | copy-start | bytes 1540
  1.6 1.2 %copy-start = (bf16[512,1024]{1,0:T(8,128)(2,1)S(1)}, bf16[512,1024]{1,0:T(8,128)(2,1)}, u32[]{:S(2)}) copy-start(bf16[512,1024]{1,0:T(8,128)(2,1)} %table_ref.1) | copy-start | bytes 3145732
  2.8 0.9 %copy-start.1 = (bf16[128,1024]{1,0:T(8,128)(2,1)S(1)}, bf16[128,1024]{1,0:T(8,128)(2,1)}, u32[]{:S(2)}) copy-start(bf16[128,1024]{1,0:T(8,128)(2,1)} %gate_ref.1) | copy-start | bytes 786436
  3.7 0.9 %copy-start.2 = (bf16[128,1024]{1,0:T(8,128)(2,1)S(1)}, bf16[128,1024]{1,0:T(8,128)(2,1)}, u32[]{:S(2)}) copy-start(bf16[128,1024]{1,0:T(8,128)(2,1)} %key_ref.1) | copy-start | bytes 786436
  4.7 0.9 %copy-start.3 = (bf16[128,1024]{1,0:T(8,128)(2,1)S(1)}, bf16[128,1024]{1,0:T(8,128)(2,1)}, u32[]{:S(2)}) copy-start(bf16[128,1024]{1,0:T(8,128)(2,1)} %attn_query_ref.1) | copy-start | bytes 786436
  5.6 0.9 %copy-start.4 = (bf16[128,1024]{1,0:T(8,128)(2,1)S(1)}, bf16[128,1024]{1,0:T(8,128)(2,1)}, u32[]{:S(2)}) copy-start(bf16[128,1024]{1,0:T(8,128)(2,1)} %attn_key_ref.1) | copy-start | bytes 786436

commit v2 on v1

--- a/solution.py
+++ b/solution.py
@@ -44,6 +44,17 @@
 
 
 def kernel(
+    ids_hbm,
+    docs_hbm,
+    table_hbm,
+    gain_hbm,
+    gate_hbm,
+    key_hbm,
+    filter_hbm,
+    attn_query_ref,
+    attn_key_ref,
+    hyena_out_ref,
+    attn_out_ref,
     ids_ref,
     docs_ref,
     table_ref,
@@ -51,10 +62,6 @@
     gate_ref,
     key_ref,
     filter_ref,
-    attn_query_ref,
-    attn_key_ref,
-    hyena_out_ref,
-    attn_out_ref,
     squares,
     meta_out,
     meta_in,
@@ -65,7 +72,6 @@
     toeplitz,
     sums,
     values_t,
-    values,
     keys,
     queries,
     docs_row,
@@ -75,6 +81,8 @@
     send,
     recv,
     local,
+    key_recv,
+    query_recv,
 ):
     me = lax.axis_index("ctx")
     my_ch = lax.axis_index("ch")
@@ -82,12 +90,12 @@
     mine = lax.div(me, 2)
     pair = me + 1 - 2 * core
 
-    def remote(src, dst, kind, to):
+    def remote(src, dst, kind, to, arrived=None):
         return pltpu.make_async_remote_copy(
             src_ref=src,
             dst_ref=dst,
             send_sem=send.at[kind],
-            recv_sem=recv.at[kind],
+            recv_sem=recv.at[kind] if arrived is None else arrived,
             device_id=to,
             device_id_type=MESH,
         )
@@ -97,6 +105,28 @@
 
     def wait_out(ref, kind):
         pltpu.make_async_copy(ref, ref, send.at[kind]).wait()
+
+    loads = [
+        pltpu.make_async_copy(src, dst, local.at[at])
+        for at, (src, dst) in enumerate(
+            (
+                (table_hbm, table_ref),
+                (filter_hbm, filter_ref),
+                (docs_hbm, docs_ref),
+                (ids_hbm, ids_ref),
+                (key_hbm, key_ref),
+                (gain_hbm, gain_ref),
+                (gate_hbm, gate_ref),
+            )
+        )
+    ]
+    for load in loads:
+        load.start()
+
+    my_keys = keys.at[pl.ds(PAD + me * ROWS, ROWS)]
+    my_head = pl.ds(pl.multiple_of(lax.div(me, 4) * HEAD_DIM, HEAD_DIM), HEAD_DIM)
+    pltpu.make_async_copy(attn_key_ref.at[:, my_head], my_keys, key_recv.at[0]).start()
+    pltpu.make_async_copy(attn_query_ref.at[:, my_head], queries.at[mine], query_recv.at[0]).start()
 
     barrier = pltpu.get_barrier_semaphore()
 
@@ -110,6 +140,9 @@
         pl.semaphore_signal(
             barrier, inc=1, device_id={"ch": lax.rem(my_ch + r, CH)}, device_id_type=MESH
         )
+
+    for load in loads:
+        load.wait()
 
     by_lane = jnp.zeros((VOCAB, 128), F32)
     for tile in range(WIDTH // 128):
@@ -119,12 +152,22 @@
     ones = jnp.ones((8, 128), BF16)
     squares[my_ch] = nt_dot(ones, high) + nt_dot(ones, low)
 
-    taps = jnp.concatenate([filter_ref[...], jnp.zeros((ROWS, 64), F32)], axis=1).T
+    taps = filter_ref[...]
     docs = docs_ref[...].astype(F32)
     for d in range(CTX):
         meta_out[d] = jnp.concatenate([taps[2 * d : 2 * d + 2], docs, docs], axis=0)
     meta_in[me] = meta_out[me]
 
+    gate_out[...] = gate_ref[...].astype(F32).T.astype(BF16).reshape(CTX, OWN, ROWS)
+    gate_in[me] = gate_out[me]
+    docs_row[:, 0:PAD] = jnp.full((8, PAD), -1.0, F32)
+    keys[0:PAD] = jnp.zeros((PAD, 128), BF16)
+    values_t[0:64, 0:PAD] = jnp.zeros((64, PAD), BF16)
+    values_t[64:80, :] = jnp.ones((16, PAD + CTX * ROWS), BF16)
+    one_hot_t = (lax.broadcasted_iota(jnp.int32, (VOCAB, ROWS), 0) == ids_ref[...]).astype(F32)
+    picked = nn_dot(one_hot_t.T.astype(BF16), table_ref[...])
+    product_t = (picked * key_ref[...].astype(F32) * gain_ref[...]).T
+
     pl.semaphore_wait(barrier, CTX - 1 + CH - 1)
 
     for r in range(1, CH):
@@ -135,10 +178,6 @@
     def _(r):
         to = lax.rem(me + r, CTX)
         remote(meta_out.at[to], meta_in.at[me], META, {"ctx": to}).start()
-
-    one_hot_t = (lax.broadcasted_iota(jnp.int32, (VOCAB, ROWS), 0) == ids_ref[...]).astype(F32)
-    picked = nn_dot(one_hot_t.T.astype(BF16), table_ref[...])
-    product_t = (picked * key_ref[...].astype(F32) * gain_ref[...]).T
 
     wait_in(squares.at[pl.ds(0, CH - 1)], SQUARES)
     total = squares[0] + squares[1] + squares[2] + squares[3]
@@ -154,32 +193,24 @@
         to = lax.rem(me + r, CTX)
         remote(source_out.at[to], source_in.at[me], SOURCE, {"ctx": to}).start()
 
-    gate_out[...] = gate_ref[...].astype(F32).T.astype(BF16).reshape(CTX, OWN, ROWS)
-    gate_in[me] = gate_out[me]
-
     @pl.loop(1, CTX)
     def _(r):
         to = lax.rem(me + r, CTX)
         remote(gate_out.at[to], gate_in.at[me], GATE, {"ctx": to}).start()
 
-    my_keys = keys.at[pl.ds(PAD + me * ROWS, ROWS)]
-    my_head = pl.ds(pl.multiple_of(lax.div(me, 4) * HEAD_DIM, HEAD_DIM), HEAD_DIM)
-    own_key = pltpu.make_async_copy(attn_key_ref.at[:, my_head], my_keys, local.at[0])
-    own_query = pltpu.make_async_copy(attn_query_ref.at[:, my_head], queries.at[mine], local.at[1])
-    own_key.start()
-    own_query.start()
-
     @pl.loop(1, CTX // 2)
     def _(r):
         to = lax.rem(me + 2 * r, CTX)
         head = pl.ds(pl.multiple_of(lax.div(to, 4) * HEAD_DIM, HEAD_DIM), HEAD_DIM)
-        remote(attn_key_ref.at[:, head], my_keys, KEY, {"ctx": to}).start()
+        remote(attn_key_ref.at[:, head], my_keys, KEY, {"ctx": to}, key_recv.at[r]).start()
 
     @pl.loop(1, CTX // 2)
     def _(r):
         to = lax.rem(me + 2 * r, CTX)
         head = pl.ds(pl.multiple_of(lax.div(to, 4) * HEAD_DIM, HEAD_DIM), HEAD_DIM)
-        remote(attn_query_ref.at[:, head], queries.at[mine], QUERY, {"ctx": to}).start()
+        remote(
+            attn_query_ref.at[:, head], queries.at[mine], QUERY, {"ctx": to}, query_recv.at[r]
+        ).start()
 
     wait_in(meta_in.at[pl.ds(0, CTX - 1)], META)
     down = lax.broadcasted_iota(jnp.int32, (ROWS, ROWS), 0)
@@ -208,13 +239,10 @@
             0, 16, build, (jnp.zeros((ROWS, ROWS), F32), jnp.zeros((ROWS, ROWS), BF16))
         )
 
-    docs_row[:, 0:PAD] = jnp.full((8, PAD), -1.0, F32)
     for j in range(CTX):
         docs_row[:, PAD + j * ROWS : PAD + (j + 1) * ROWS] = jnp.broadcast_to(
             meta_in[j, 2:3, :], (8, ROWS)
         )
-    values[0:PAD] = jnp.zeros((PAD, 128), BF16)
-    keys[0:PAD] = jnp.zeros((PAD, 128), BF16)
 
     wait_in(source_in.at[pl.ds(0, CTX - 1)], SOURCE)
     for g in range(2):
@@ -230,74 +258,71 @@
     wait_in(gate_in.at[pl.ds(0, CTX - 1)], GATE)
     for g in range(2):
         own = slice(g * GROUP, (g + 1) * GROUP)
-        convolved = jnp.stack(
-            [sums[g, :, half * ROWS : (half + 1) * ROWS].reshape(16, GROUP, ROWS) for half in range(2)],
-            axis=1,
-        ).reshape(CTX, GROUP, ROWS)
-        values_t[core, :, own, :] = (convolved * gate_in[:, own, :].astype(F32)).astype(BF16)
-
-    remote(values_t.at[core], values_t.at[core], VALUE_PAIR, {"ctx": pair}).start()
-
-    own_key.wait()
-    own_query.wait()
-    wait_in(keys.at[pl.ds(0, 15 * ROWS)], KEY)
-
-    @pl.loop(0, 16)
-    def _(q):
-        block = keys.at[pl.ds(PAD + (2 * q + core) * ROWS, ROWS)]
+        rows = pl.ds(pl.multiple_of(OWN * core + GROUP * g, GROUP), GROUP)
+        for j in range(16):
+            gate = jnp.concatenate([gate_in[2 * j, own, :], gate_in[2 * j + 1, own, :]], axis=1)
+            gated = sums[g, 16 * j : 16 * (j + 1)] * gate.astype(F32)
+            values_t[rows, PAD + 256 * j : PAD + 256 * (j + 1)] = gated.astype(BF16)
+
+    my_rows = pl.ds(pl.multiple_of(OWN * core, OWN), OWN)
+    my_values = values_t.at[my_rows, pl.ds(PAD, CTX * ROWS)]
+    remote(my_values, my_values, VALUE_PAIR, {"ctx": pair}).start()
+
+    @pl.loop(0, CTX // 2)
+    def _(r):
+        source = lax.rem(me + CTX - 2 * r, CTX)
+        block = keys.at[pl.ds(PAD + source * ROWS, ROWS)]
+        pltpu.make_async_copy(block, block, key_recv.at[r]).wait()
         remote(block, block, KEY_PAIR, {"ctx": pair}).start()
 
     @pl.loop(1, CTX)
     def _(r):
         to = lax.rem(me + r, CTX)
-        block = values_t.at[core, to]
+        block = values_t.at[my_rows, pl.ds(pl.multiple_of(PAD + to * ROWS, ROWS), ROWS)]
         remote(block, home_in.at[me], HOME, {"ctx": to}).start()
 
-    home_in[me] = values_t[core, me]
-
-    wait_in(queries.at[pl.ds(0, 15)], QUERY)
-    wait_in(values_t.at[0], VALUE_PAIR)
-
-    @pl.loop(0, CTX)
-    def _(j):
-        block = jnp.concatenate(
-            [
-                values_t[0, j].astype(F32),
-                values_t[1, j].astype(F32),
-                jnp.ones((64, ROWS), F32),
-            ],
-            axis=0,
-        )
-        values[pl.ds(pl.multiple_of(PAD + j * ROWS, ROWS), ROWS)] = block.T.astype(BF16)
-
+    home_in[me] = values_t[my_rows, pl.ds(pl.multiple_of(PAD + me * ROWS, ROWS), ROWS)]
+
+    wait_in(source_in, VALUE_PAIR)
     wait_in(keys.at[pl.ds(0, 16 * ROWS)], KEY_PAIR)
 
-    @pl.loop(0, 16)
-    def _(q):
-        block = 2 * q + core
-        start = pl.multiple_of(block * ROWS, ROWS)
+    def attend(q):
+        start = pl.multiple_of((2 * q + core) * ROWS, ROWS)
         window = pl.ds(start, WINDOW)
         scores = nt_dot(queries[q], keys[window])
         own_docs = docs_row[0:1, pl.ds(pl.multiple_of(PAD + start, ROWS), ROWS)]
         own_docs = jnp.broadcast_to(own_docs, (ROWS, ROWS)).T[:, 0:1]
-        allowed = docs_row[0:1, window] == own_docs
-        causal = lax.broadcasted_iota(jnp.int32, (ROWS, WINDOW), 1) <= PAD + (
-            lax.broadcasted_iota(jnp.int32, (ROWS, WINDOW), 0)
-        )
-        scores = jnp.where(allowed & causal, scores, MASKED)
+        same = docs_row[0:1, window] == own_docs
+        past = jnp.where(same[:, :PAD], scores[:, :PAD], MASKED)
+        diagonal = jnp.where(same[:, PAD:] & (down >= right), scores[:, PAD:], MASKED)
+        scores = jnp.concatenate([past, diagonal], axis=1)
         top = jnp.max(scores, axis=1, keepdims=True)
         weights = jnp.exp2((scores - top) * EXPONENT).astype(BF16)
-        numerator = nn_dot(weights, values[window])
-        result = numerator * (1.0 / numerator[:, 64:65])
-        attn_t[q] = result.T[0:64].astype(BF16)
-
-        @pl.when(block != me)
+        numerator = nt_dot(values_t[:, window], weights)
+        attn_t[q] = (numerator[0:64] * (1.0 / numerator[64:65])).astype(BF16)
+
+    def give(q):
+        block = 2 * q + core
+        remote(attn_t.at[q], attn_in.at[mine], ATTN, {"ctx": block}).start()
+
+    @pl.loop(0, 8)
+    def _(p):
+        places = [lax.rem(mine + 16 - 2 * p - at, 16) for at in range(2)]
+        for at in range(2):
+            block = queries.at[places[at]]
+            pltpu.make_async_copy(block, block, query_recv.at[2 * p + at]).wait()
+        for at in range(2):
+            attend(places[at])
+
+        @pl.when(p == 0)
         def _():
-            remote(attn_t.at[q], attn_in.at[mine], ATTN, {"ctx": block}).start()
-
-        @pl.when(block == me)
+            attn_in[mine] = attn_t[mine]
+
+        @pl.when(p > 0)
         def _():
-            attn_in[mine] = attn_t[q]
+            give(places[0])
+
+        give(places[1])
 
     wait_in(home_in.at[pl.ds(0, CTX - 1)], HOME)
     hyena_out_ref[...] = home_in[...].reshape(WIDTH, ROWS).astype(F32).T.astype(BF16)
@@ -311,7 +336,7 @@
     wait_out(queries.at[pl.ds(0, 15)], QUERY)
     wait_out(keys.at[pl.ds(0, 15 * ROWS)], KEY)
     wait_out(keys.at[pl.ds(0, 16 * ROWS)], KEY_PAIR)
-    wait_out(values_t.at[0], VALUE_PAIR)
+    wait_out(source_in, VALUE_PAIR)
     wait_out(home_in.at[pl.ds(0, CTX - 1)], HOME)
     wait_out(attn_in.at[pl.ds(0, 15)], ATTN)
 
@@ -333,9 +358,16 @@
     return pl.pallas_call(
         kernel,
         out_shape=(shape, shape),
-        in_specs=[vmem] * 7 + [hbm] * 2,
+        in_specs=[hbm] * 9,
         out_specs=(vmem, vmem),
         scratch_shapes=[
+            pltpu.VMEM((1, ROWS), jnp.int32),
+            pltpu.VMEM((1, ROWS), jnp.int32),
+            pltpu.VMEM((VOCAB, WIDTH), BF16),
+            pltpu.VMEM((1, WIDTH), F32),
+            pltpu.VMEM((ROWS, WIDTH), BF16),
+            pltpu.VMEM((ROWS, WIDTH), BF16),
+            pltpu.VMEM((64, ROWS), F32),
             pltpu.VMEM((CH, 8, VOCAB), F32),
             pltpu.VMEM((CTX, 4, ROWS), F32),
             pltpu.VMEM((CTX, 4, ROWS), F32),
@@ -345,8 +377,7 @@
             pltpu.VMEM((CTX, OWN, ROWS), BF16),
             pltpu.VMEM((2, 16, 256, 256), BF16),
             pltpu.VMEM((2, 256, 256), F32),
-            pltpu.VMEM((2, CTX, OWN, ROWS), BF16),
-            pltpu.VMEM((PAD + CTX * ROWS, 128), BF16),
+            pltpu.VMEM((80, PAD + CTX * ROWS), BF16),
             pltpu.VMEM((PAD + CTX * ROWS, 128), BF16),
             pltpu.VMEM((16, ROWS, HEAD_DIM), BF16),
             pltpu.VMEM((8, PAD + CTX * ROWS), F32),
@@ -355,10 +386,12 @@
             pltpu.VMEM((16, 64, ROWS), BF16),
             pltpu.SemaphoreType.DMA((10,)),
             pltpu.SemaphoreType.DMA((10,)),
-            pltpu.SemaphoreType.DMA((2,)),
+            pltpu.SemaphoreType.DMA((7,)),
+            pltpu.SemaphoreType.DMA((CTX // 2,)),
+            pltpu.SemaphoreType.DMA((CTX // 2,)),
         ],
         compiler_params=pltpu.CompilerParams(
-            collective_id=0, has_side_effects=True, vmem_limit_bytes=48 * 1024 * 1024
+            collective_id=0, has_side_effects=True, vmem_limit_bytes=60 * 1024 * 1024
         ),
     )(
         token_ids.reshape(1, ROWS),
@@ -367,7 +400,7 @@
         norm_gain.reshape(1, WIDTH),
         hyena_query,
         hyena_key,
-        hyena_filter,
+        hyena_filter.T,
         attn_query,
         attn_key,
     )

time: 60 us -> 52 us (0.87)
  the two profiles are of different devices: /device:TPU:24 before, /device:TPU:1 now
where the time goes in v2:
time: 52 us; the launch traced here: 51.8 us
  Pallas kernels  48.7 us (94%)
  local copies, waits for them, and re-layouts  2.42 us (5%)
  between operations  0.65 us (1%)
    pallas_call x1, Pallas kernels, per_device(): pl.pallas_call(kernel, out_shape=(shape, shape), in_specs=[hbm] * 9, out_...  48.7 us
    unnamed x4, local copies, waits for them, and re-layouts  2.42 us

profile of v2, /device:TPU:1, one launch (start us, length us, event | category | flops | bytes accessed | tf_op | source)
XLA Modules:
  0.0 51.8 jit_solution(10829829439390047308)
XLA Ops:
  0.6 48.7 %shard_map.104 = (bf16[128,1024]{1,0:T(8,128)(2,1)}, bf16[128,1024]{1,0:T(8,128)(2,1)}) custom-call(s32[1,128]{1,0:T(1,128)} %bitcast.6, s32[1,128]{1,0:T(1,128)} %bitcast.7, bf16[512,1024]{1,0:T(8,128)(2,1)} %table_hbm.1, f32[1,1024]{1,0:T(1,128)} %bitcast.5, bf16[128,1024]{1,0:T(8,128)(2,1)} %gate_hbm.1, bf16[128,1024]{1,0:T(8,128)(2,1)} %key_hbm.1, ...), custom_call_target="tpu_custom_call" | custom-call | tf_op jit(solution)/shard_map/pallas_call | solution.py:358
  49.4 0.0 copy-start
  49.4 1.7 %copy.13 = bf16[128,1024]{1,0:T(8,128)(2,1)} copy(bf16[128,1024]{1,0:T(8,128)(2,1)} %get-tuple-element.4) | data formatting | bytes 524288
  51.1 0.0 copy-done
  51.1 0.7 %copy.14 = bf16[128,1024]{1,0:T(8,128)(2,1)} copy(bf16[128,1024]{1,0:T(8,128)(2,1)S(1)} %copy-done) | data formatting | bytes 524288
Async XLA Ops:
  49.4 1.7 %copy-start = (bf16[128,1024]{1,0:T(8,128)(2,1)S(1)}, bf16[128,1024]{1,0:T(8,128)(2,1)}, u32[]{:S(2)}) copy-start(bf16[128,1024]{1,0:T(8,128)(2,1)} %get-tuple-element.5) | copy-start | bytes 786436

commit v3 on v2

--- a/solution.py
+++ b/solution.py
@@ -21,10 +21,10 @@
 OWN = 32
 GROUP = 16
 HEAD_DIM = 128
-PAD = 2048
-WINDOW = PAD + ROWS
+REACH = 2048
 EPSILON = 1e-06
 MASKED = -1e30
+SAME = 8192.0
 EXPONENT = HEAD_DIM**-0.5 * math.log2(math.e)
 
 META, SOURCE, GATE, QUERY, KEY, KEY_PAIR, VALUE_PAIR, HOME, ATTN, SQUARES = range(10)
@@ -63,6 +63,9 @@
     key_ref,
     filter_ref,
     squares,
+    ids_row,
+    scales,
+    signals,
     meta_out,
     meta_in,
     source_out,
@@ -73,8 +76,9 @@
     sums,
     values_t,
     keys,
+    key_docs,
     queries,
-    docs_row,
+    query_docs,
     home_in,
     attn_t,
     attn_in,
@@ -123,10 +127,11 @@
     for load in loads:
         load.start()
 
-    my_keys = keys.at[pl.ds(PAD + me * ROWS, ROWS)]
+    my_keys = keys.at[pl.ds(me * ROWS, ROWS)]
+    my_queries = queries.at[mine]
     my_head = pl.ds(pl.multiple_of(lax.div(me, 4) * HEAD_DIM, HEAD_DIM), HEAD_DIM)
     pltpu.make_async_copy(attn_key_ref.at[:, my_head], my_keys, key_recv.at[0]).start()
-    pltpu.make_async_copy(attn_query_ref.at[:, my_head], queries.at[mine], query_recv.at[0]).start()
+    pltpu.make_async_copy(attn_query_ref.at[:, my_head], my_queries, query_recv.at[0]).start()
 
     barrier = pltpu.get_barrier_semaphore()
 
@@ -141,8 +146,33 @@
             barrier, inc=1, device_id={"ch": lax.rem(my_ch + r, CH)}, device_id_type=MESH
         )
 
-    for load in loads:
+    for load in loads[:6]:
         load.wait()
+
+    taps = filter_ref[...]
+    docs = docs_ref[...].astype(F32)
+    ids = ids_ref[...].astype(F32)
+    for d in range(CTX):
+        meta_out[d] = jnp.concatenate([taps[2 * d : 2 * d + 2], docs, ids], axis=0)
+    meta_in[me] = meta_out[me]
+
+    one_hot_t = (lax.broadcasted_iota(jnp.int32, (VOCAB, ROWS), 0) == ids_ref[...]).astype(F32)
+    picked = nn_dot(one_hot_t.T.astype(BF16), table_ref[...])
+    product = picked * key_ref[...].astype(F32) * gain_ref[...]
+    source_out[...] = product.T.astype(BF16).reshape(CTX, OWN, ROWS)
+    source_in[me] = source_out[me]
+
+    pl.semaphore_wait(barrier, CTX - 1 + CH - 1)
+
+    @pl.loop(1, CTX)
+    def _(r):
+        to = lax.rem(me + r, CTX)
+        remote(meta_out.at[to], meta_in.at[me], META, {"ctx": to}).start()
+
+    @pl.loop(1, CTX)
+    def _(r):
+        to = lax.rem(me + r, CTX)
+        remote(source_out.at[to], source_in.at[me], SOURCE, {"ctx": to}).start()
 
     by_lane = jnp.zeros((VOCAB, 128), F32)
     for tile in range(WIDTH // 128):
@@ -152,46 +182,13 @@
     ones = jnp.ones((8, 128), BF16)
     squares[my_ch] = nt_dot(ones, high) + nt_dot(ones, low)
 
-    taps = filter_ref[...]
-    docs = docs_ref[...].astype(F32)
-    for d in range(CTX):
-        meta_out[d] = jnp.concatenate([taps[2 * d : 2 * d + 2], docs, docs], axis=0)
-    meta_in[me] = meta_out[me]
-
-    gate_out[...] = gate_ref[...].astype(F32).T.astype(BF16).reshape(CTX, OWN, ROWS)
-    gate_in[me] = gate_out[me]
-    docs_row[:, 0:PAD] = jnp.full((8, PAD), -1.0, F32)
-    keys[0:PAD] = jnp.zeros((PAD, 128), BF16)
-    values_t[0:64, 0:PAD] = jnp.zeros((64, PAD), BF16)
-    values_t[64:80, :] = jnp.ones((16, PAD + CTX * ROWS), BF16)
-    one_hot_t = (lax.broadcasted_iota(jnp.int32, (VOCAB, ROWS), 0) == ids_ref[...]).astype(F32)
-    picked = nn_dot(one_hot_t.T.astype(BF16), table_ref[...])
-    product_t = (picked * key_ref[...].astype(F32) * gain_ref[...]).T
-
-    pl.semaphore_wait(barrier, CTX - 1 + CH - 1)
-
     for r in range(1, CH):
         to = lax.rem(my_ch + r, CH)
         remote(squares.at[my_ch], squares.at[my_ch], SQUARES, {"ch": to}).start()
 
-    @pl.loop(1, CTX)
-    def _(r):
-        to = lax.rem(me + r, CTX)
-        remote(meta_out.at[to], meta_in.at[me], META, {"ctx": to}).start()
-
-    wait_in(squares.at[pl.ds(0, CH - 1)], SQUARES)
-    total = squares[0] + squares[1] + squares[2] + squares[3]
-    high, low = halves(total)
-    one_hot_t = one_hot_t.astype(BF16)
-    mean_square = (nn_dot(high, one_hot_t) + nn_dot(low, one_hot_t)) * (1.0 / CHANNELS)
-    scale = lax.rsqrt(mean_square + EPSILON)[0:1]
-    source_out[...] = (product_t * scale).astype(BF16).reshape(CTX, OWN, ROWS)
-    source_in[me] = source_out[me]
-
-    @pl.loop(1, CTX)
-    def _(r):
-        to = lax.rem(me + r, CTX)
-        remote(source_out.at[to], source_in.at[me], SOURCE, {"ctx": to}).start()
+    loads[6].wait()
+    gate_out[...] = gate_ref[...].astype(F32).T.astype(BF16).reshape(CTX, OWN, ROWS)
+    gate_in[me] = gate_out[me]
 
     @pl.loop(1, CTX)
     def _(r):
@@ -209,8 +206,10 @@
         to = lax.rem(me + 2 * r, CTX)
         head = pl.ds(pl.multiple_of(lax.div(to, 4) * HEAD_DIM, HEAD_DIM), HEAD_DIM)
         remote(
-            attn_query_ref.at[:, head], queries.at[mine], QUERY, {"ctx": to}, query_recv.at[r]
+            attn_query_ref.at[:, head], my_queries, QUERY, {"ctx": to}, query_recv.at[r]
         ).start()
+
+    values_t[64:80, :] = jnp.ones((16, CTX * ROWS), BF16)
 
     wait_in(meta_in.at[pl.ds(0, CTX - 1)], META)
     down = lax.broadcasted_iota(jnp.int32, (ROWS, ROWS), 0)
@@ -239,18 +238,49 @@
             0, 16, build, (jnp.zeros((ROWS, ROWS), F32), jnp.zeros((ROWS, ROWS), BF16))
         )
 
+    @pl.loop(0, CTX)
+    def _(j):
+        which = down.astype(F32) == meta_in[j, 2:3, :]
+        key_docs[pl.ds(pl.multiple_of(j * ROWS, ROWS), ROWS)] = (
+            which.astype(F32).T.astype(BF16)
+        )
+
+    @pl.loop(0, 16)
+    def _(q):
+        rows = pl.ds(pl.multiple_of((2 * q + core) * ROWS, ROWS), ROWS)
+        query_docs[q] = (key_docs[rows].astype(F32) * SAME).astype(BF16)
+
     for j in range(CTX):
-        docs_row[:, PAD + j * ROWS : PAD + (j + 1) * ROWS] = jnp.broadcast_to(
-            meta_in[j, 2:3, :], (8, ROWS)
-        )
+        ids_row[:, j * ROWS : (j + 1) * ROWS] = meta_in[j, 3:4, :].astype(jnp.int32)
+    wait_in(squares.at[pl.ds(0, CH - 1)], SQUARES)
+    total = (squares[0] + squares[1] + squares[2] + squares[3])[0:1]
+    low_digit = lax.broadcasted_iota(jnp.int32, (16, VOCAB), 0)
+    token = lax.broadcasted_iota(jnp.int32, (16, VOCAB), 1)
+    high, low = halves(jnp.where(lax.rem(token, 16) == low_digit, total, 0.0))
+    high_digit = lax.broadcasted_iota(jnp.int32, (32, VOCAB), 0)
+    token = lax.broadcasted_iota(jnp.int32, (32, VOCAB), 1)
+    gather = (lax.div(token, 16) == high_digit).astype(F32).astype(BF16)
+    high, low = halves(nt_dot(high, gather) + nt_dot(low, gather))
+    digits = lax.div(ids_row[...], 16)
+    chosen = lax.broadcasted_iota(jnp.int32, (32, CTX * ROWS), 0) == digits
+    chosen = chosen.astype(F32).astype(BF16)
+    choices = nn_dot(high, chosen) + nn_dot(low, chosen)
+    digits = lax.rem(ids_row[...], 16)
+    chosen = lax.broadcasted_iota(jnp.int32, (16, CTX * ROWS), 0) == digits
+    square = jnp.sum(jnp.where(chosen, choices, 0.0), axis=0, keepdims=True)
+    scales[...] = lax.rsqrt(square * (1.0 / CHANNELS) + EPSILON)
 
     wait_in(source_in.at[pl.ds(0, CTX - 1)], SOURCE)
+    for j in range(CTX):
+        scaled = source_in[j].astype(F32) * scales[:, j * ROWS : (j + 1) * ROWS]
+        scaled = scaled.astype(BF16)
+        lanes = slice(j % 2 * ROWS, (j % 2 + 1) * ROWS)
+        for g in range(2):
+            signals[g, j // 2 * GROUP : (j // 2 + 1) * GROUP, lanes] = scaled[
+                g * GROUP : (g + 1) * GROUP
+            ]
     for g in range(2):
-        own = slice(g * GROUP, (g + 1) * GROUP)
-        signal = source_in[:, own, :].reshape(16, 2, GROUP, ROWS)
-        signal = jnp.concatenate(
-            [signal[:, half].reshape(256, ROWS) for half in range(2)], axis=1
-        )
+        signal = signals[g]
         sums[g] = nn_dot(signal, toeplitz[g, 0])
         for k in range(1, 16):
             sums[g, 16 * k :] += nn_dot(signal[: 256 - 16 * k], toeplitz[g, k])
@@ -262,67 +292,83 @@
         for j in range(16):
             gate = jnp.concatenate([gate_in[2 * j, own, :], gate_in[2 * j + 1, own, :]], axis=1)
             gated = sums[g, 16 * j : 16 * (j + 1)] * gate.astype(F32)
-            values_t[rows, PAD + 256 * j : PAD + 256 * (j + 1)] = gated.astype(BF16)
+            values_t[rows, 256 * j : 256 * (j + 1)] = gated.astype(BF16)
 
     my_rows = pl.ds(pl.multiple_of(OWN * core, OWN), OWN)
-    my_values = values_t.at[my_rows, pl.ds(PAD, CTX * ROWS)]
+    my_values = values_t.at[my_rows, pl.ds(0, CTX * ROWS)]
     remote(my_values, my_values, VALUE_PAIR, {"ctx": pair}).start()
 
     @pl.loop(0, CTX // 2)
     def _(r):
         source = lax.rem(me + CTX - 2 * r, CTX)
-        block = keys.at[pl.ds(PAD + source * ROWS, ROWS)]
+        block = keys.at[pl.ds(source * ROWS, ROWS)]
         pltpu.make_async_copy(block, block, key_recv.at[r]).wait()
         remote(block, block, KEY_PAIR, {"ctx": pair}).start()
 
     @pl.loop(1, CTX)
     def _(r):
         to = lax.rem(me + r, CTX)
-        block = values_t.at[my_rows, pl.ds(pl.multiple_of(PAD + to * ROWS, ROWS), ROWS)]
+        block = values_t.at[my_rows, pl.ds(pl.multiple_of(to * ROWS, ROWS), ROWS)]
         remote(block, home_in.at[me], HOME, {"ctx": to}).start()
 
-    home_in[me] = values_t[my_rows, pl.ds(pl.multiple_of(PAD + me * ROWS, ROWS), ROWS)]
+    home_in[me] = values_t[my_rows, pl.ds(pl.multiple_of(me * ROWS, ROWS), ROWS)]
 
     wait_in(source_in, VALUE_PAIR)
     wait_in(keys.at[pl.ds(0, 16 * ROWS)], KEY_PAIR)
 
-    def attend(q):
-        start = pl.multiple_of((2 * q + core) * ROWS, ROWS)
-        window = pl.ds(start, WINDOW)
-        scores = nt_dot(queries[q], keys[window])
-        own_docs = docs_row[0:1, pl.ds(pl.multiple_of(PAD + start, ROWS), ROWS)]
-        own_docs = jnp.broadcast_to(own_docs, (ROWS, ROWS)).T[:, 0:1]
-        same = docs_row[0:1, window] == own_docs
-        past = jnp.where(same[:, :PAD], scores[:, :PAD], MASKED)
-        diagonal = jnp.where(same[:, PAD:] & (down >= right), scores[:, PAD:], MASKED)
-        scores = jnp.concatenate([past, diagonal], axis=1)
-        top = jnp.max(scores, axis=1, keepdims=True)
-        weights = jnp.exp2((scores - top) * EXPONENT).astype(BF16)
-        numerator = nt_dot(values_t[:, window], weights)
-        attn_t[q] = (numerator[0:64] * (1.0 / numerator[64:65])).astype(BF16)
+    def attend(u, start, blocks, clear):
+        rows = pl.ds(pl.multiple_of(start, ROWS), blocks * ROWS)
+        some_keys = jnp.concatenate([keys[rows], key_docs[rows]], axis=1)
+        both = pl.ds(2 * u, 2)
+        some_queries = jnp.concatenate([queries[both], query_docs[both]], axis=2)
+        scores = nt_dot(some_keys, some_queries.reshape(2 * ROWS, 256))
+        shape = ((blocks - clear) * ROWS, 2 * ROWS)
+        at_key = lax.broadcasted_iota(jnp.int32, shape, 0) + (start + clear * ROWS)
+        at_query = lax.broadcasted_iota(jnp.int32, shape, 1)
+        at_query = jnp.where(at_query >= ROWS, at_query + ROWS, at_query) + (4 * u + core) * ROWS
+        late = jnp.where(at_key <= at_query, scores[clear * ROWS :], MASKED)
+        if clear:
+            late = jnp.concatenate([scores[: clear * ROWS], late], axis=0)
+        top = jnp.max(late, axis=0, keepdims=True)
+        weights = jnp.exp2((late - top) * EXPONENT).astype(BF16)
+        numerator = nn_dot(values_t[:, rows], weights)
+        result = (numerator[0:64] * (1.0 / numerator[64:65])).astype(BF16)
+        attn_t[2 * u] = result[:, :ROWS]
+        attn_t[2 * u + 1] = result[:, ROWS:]
 
     def give(q):
         block = 2 * q + core
-        remote(attn_t.at[q], attn_in.at[mine], ATTN, {"ctx": block}).start()
+
+        @pl.when(q == mine)
+        def _():
+            attn_in[mine] = attn_t[q]
+
+        @pl.when(q != mine)
+        def _():
+            remote(attn_t.at[q], attn_in.at[mine], ATTN, {"ctx": block}).start()
 
     @pl.loop(0, 8)
     def _(p):
-        places = [lax.rem(mine + 16 - 2 * p - at, 16) for at in range(2)]
+        u = lax.rem(lax.div(mine + 1, 2) + 7 - p, 8)
         for at in range(2):
-            block = queries.at[places[at]]
-            pltpu.make_async_copy(block, block, query_recv.at[2 * p + at]).wait()
-        for at in range(2):
-            attend(places[at])
-
-        @pl.when(p == 0)
+            block = queries.at[2 * u + at]
+            arrived = query_recv.at[lax.rem(mine + 16 - 2 * u - at, 16)]
+            pltpu.make_async_copy(block, block, arrived).wait()
+
+        @pl.when(u < 2)
         def _():
-            attn_in[mine] = attn_t[mine]
-
-        @pl.when(p > 0)
+            attend(u, 0, 8, 0)
+
+        @pl.when((u >= 2) & (u < 4))
         def _():
-            give(places[0])
-
-        give(places[1])
+            attend(u, 0, 16, 8)
+
+        @pl.when(u >= 4)
+        def _():
+            attend(u, (4 * u + core) * ROWS - REACH, 19, 16)
+
+        give(2 * u)
+        give(2 * u + 1)
 
     wait_in(home_in.at[pl.ds(0, CTX - 1)], HOME)
     hyena_out_ref[...] = home_in[...].reshape(WIDTH, ROWS).astype(F32).T.astype(BF16)
@@ -369,6 +415,9 @@
             pltpu.VMEM((ROWS, WIDTH), BF16),
             pltpu.VMEM((64, ROWS), F32),
             pltpu.VMEM((CH, 8, VOCAB), F32),
+            pltpu.VMEM((1, CTX * ROWS), jnp.int32),
+            pltpu.VMEM((1, CTX * ROWS), F32),
+            pltpu.VMEM((2, 256, 256), BF16),
             pltpu.VMEM((CTX, 4, ROWS), F32),
             pltpu.VMEM((CTX, 4, ROWS), F32),
             pltpu.VMEM((CTX, OWN, ROWS), BF16),
@@ -377,10 +426,11 @@
             pltpu.VMEM((CTX, OWN, ROWS), BF16),
             pltpu.VMEM((2, 16, 256, 256), BF16),
             pltpu.VMEM((2, 256, 256), F32),
-            pltpu.VMEM((80, PAD + CTX * ROWS), BF16),
-            pltpu.VMEM((PAD + CTX * ROWS, 128), BF16),
+            pltpu.VMEM((80, CTX * ROWS), BF16),
+            pltpu.VMEM((CTX * ROWS, 128), BF16),
+            pltpu.VMEM((CTX * ROWS, 128), BF16),
             pltpu.VMEM((16, ROWS, HEAD_DIM), BF16),
-            pltpu.VMEM((8, PAD + CTX * ROWS), F32),
+            pltpu.VMEM((16, ROWS, HEAD_DIM), BF16),
             pltpu.VMEM((CTX, OWN, ROWS), BF16),
             pltpu.VMEM((16, 64, ROWS), BF16),
             pltpu.VMEM((16, 64, ROWS), BF16),

time: 52 us -> 46.3 us (0.89)
  Pallas kernels: 48.7 us -> 43.1 us
    pallas_call x1, Pallas kernels: 48.7 us -> 43.1 us  [per_device(): pl.pallas_call(kernel, out_shape=(shape, shape), in_specs=[hbm] * 9, out_...]
where the time goes in v3:
time: 46.3 us; the launch traced here: 46.1 us
  Pallas kernels  43.1 us (93%)
  local copies, waits for them, and re-layouts  2.42 us (5%)
  between operations  0.65 us (1%)
    pallas_call x1, Pallas kernels, per_device(): pl.pallas_call(kernel, out_shape=(shape, shape), in_specs=[hbm] * 9, out_...  43.1 us
    unnamed x4, local copies, waits for them, and re-layouts  2.42 us

profile of v3, /device:TPU:1, one launch (start us, length us, event | category | flops | bytes accessed | tf_op | source)
XLA Modules:
  0.0 46.1 jit_solution(11826112940804331650)
XLA Ops:
  0.6 43.1 %shard_map.104 = (bf16[128,1024]{1,0:T(8,128)(2,1)}, bf16[128,1024]{1,0:T(8,128)(2,1)}) custom-call(s32[1,128]{1,0:T(1,128)} %bitcast.6, s32[1,128]{1,0:T(1,128)} %bitcast.7, bf16[512,1024]{1,0:T(8,128)(2,1)} %table_hbm.1, f32[1,1024]{1,0:T(1,128)} %bitcast.5, bf16[128,1024]{1,0:T(8,128)(2,1)} %gate_hbm.1, bf16[128,1024]{1,0:T(8,128)(2,1)} %key_hbm.1, ...), custom_call_target="tpu_custom_call" | custom-call | tf_op jit(solution)/shard_map/pallas_call | solution.py:404
  43.7 0.0 copy-start
  43.7 1.7 %copy.13 = bf16[128,1024]{1,0:T(8,128)(2,1)} copy(bf16[128,1024]{1,0:T(8,128)(2,1)} %get-tuple-element.4) | data formatting | bytes 524288
  45.4 0.0 copy-done
  45.4 0.7 %copy.14 = bf16[128,1024]{1,0:T(8,128)(2,1)} copy(bf16[128,1024]{1,0:T(8,128)(2,1)S(1)} %copy-done) | data formatting | bytes 524288
Async XLA Ops:
  43.7 1.7 %copy-start = (bf16[128,1024]{1,0:T(8,128)(2,1)S(1)}, bf16[128,1024]{1,0:T(8,128)(2,1)}, u32[]{:S(2)}) copy-start(bf16[128,1024]{1,0:T(8,128)(2,1)} %get-tuple-element.5) | copy-start | bytes 786436

commit v4 on v3

--- a/solution.py
+++ b/solution.py
@@ -53,8 +53,8 @@
     filter_hbm,
     attn_query_ref,
     attn_key_ref,
-    hyena_out_ref,
-    attn_out_ref,
+    home_in,
+    attn_in,
     ids_ref,
     docs_ref,
     table_ref,
@@ -79,9 +79,7 @@
     key_docs,
     queries,
     query_docs,
-    home_in,
     attn_t,
-    attn_in,
     send,
     recv,
     local,
@@ -311,7 +309,10 @@
         block = values_t.at[my_rows, pl.ds(pl.multiple_of(to * ROWS, ROWS), ROWS)]
         remote(block, home_in.at[me], HOME, {"ctx": to}).start()
 
-    home_in[me] = values_t[my_rows, pl.ds(pl.multiple_of(me * ROWS, ROWS), ROWS)]
+    own_home = pltpu.make_async_copy(
+        values_t.at[my_rows, pl.ds(pl.multiple_of(me * ROWS, ROWS), ROWS)], home_in.at[me], local.at[0]
+    )
+    own_home.start()
 
     wait_in(source_in, VALUE_PAIR)
     wait_in(keys.at[pl.ds(0, 16 * ROWS)], KEY_PAIR)
@@ -341,7 +342,7 @@
 
         @pl.when(q == mine)
         def _():
-            attn_in[mine] = attn_t[q]
+            pltpu.make_async_copy(attn_t.at[q], attn_in.at[mine], local.at[1]).start()
 
         @pl.when(q != mine)
         def _():
@@ -371,10 +372,10 @@
         give(2 * u + 1)
 
     wait_in(home_in.at[pl.ds(0, CTX - 1)], HOME)
-    hyena_out_ref[...] = home_in[...].reshape(WIDTH, ROWS).astype(F32).T.astype(BF16)
     wait_in(attn_in.at[pl.ds(0, 15)], ATTN)
-    attn_out_ref[...] = attn_in[...].reshape(WIDTH, ROWS).astype(F32).T.astype(BF16)
-
+
+    own_home.wait()
+    pltpu.make_async_copy(attn_t.at[mine], attn_in.at[mine], local.at[1]).wait()
     wait_out(squares.at[pl.ds(0, CH - 1)], SQUARES)
     wait_out(meta_in.at[pl.ds(0, CTX - 1)], META)
     wait_out(source_out.at[pl.ds(0, CTX - 1)], SOURCE)
@@ -385,6 +386,11 @@
     wait_out(source_in, VALUE_PAIR)
     wait_out(home_in.at[pl.ds(0, CTX - 1)], HOME)
     wait_out(attn_in.at[pl.ds(0, 15)], ATTN)
+
+
+def turn(home_ref, attn_ref, hyena_out_ref, attn_out_ref):
+    hyena_out_ref[...] = home_ref[...].astype(F32).T.astype(BF16)
+    attn_out_ref[...] = attn_ref[...].astype(F32).T.astype(BF16)
 
 
 def per_device(
@@ -399,13 +405,16 @@
     document_ids,
 ):
     vmem = pl.BlockSpec(memory_space=pltpu.VMEM)
-    hbm = pl.BlockSpec(memory_space=pl.ANY)
+    hbm = pl.BlockSpec(memory_space=pltpu.HBM)
     shape = jax.ShapeDtypeStruct((ROWS, WIDTH), BF16)
-    return pl.pallas_call(
+    sent = pl.pallas_call(
         kernel,
-        out_shape=(shape, shape),
+        out_shape=(
+            jax.ShapeDtypeStruct((CTX, OWN, ROWS), BF16),
+            jax.ShapeDtypeStruct((16, 64, ROWS), BF16),
+        ),
         in_specs=[hbm] * 9,
-        out_specs=(vmem, vmem),
+        out_specs=(hbm, hbm),
         scratch_shapes=[
             pltpu.VMEM((1, ROWS), jnp.int32),
             pltpu.VMEM((1, ROWS), jnp.int32),
@@ -431,8 +440,6 @@
             pltpu.VMEM((CTX * ROWS, 128), BF16),
             pltpu.VMEM((16, ROWS, HEAD_DIM), BF16),
             pltpu.VMEM((16, ROWS, HEAD_DIM), BF16),
-            pltpu.VMEM((CTX, OWN, ROWS), BF16),
-            pltpu.VMEM((16, 64, ROWS), BF16),
             pltpu.VMEM((16, 64, ROWS), BF16),
             pltpu.SemaphoreType.DMA((10,)),
             pltpu.SemaphoreType.DMA((10,)),
@@ -454,6 +461,12 @@
         attn_query,
         attn_key,
     )
+    return pl.pallas_call(
+        turn,
+        out_shape=(shape, shape),
+        in_specs=[vmem] * 2,
+        out_specs=(vmem, vmem),
+    )(*(part.reshape(WIDTH, ROWS) for part in sent))
 
 
 def solution(mesh):

time: 46.3 us -> 45 us (0.972)
  local copies, waits for them, and re-layouts: 2.42 us -> 0 us
  Pallas kernels: 43.1 us -> 44.2 us
    unnamed x4 -> x0, local copies, waits for them, and re-layouts: 2.42 us -> none
    pallas_call x1 -> x2, Pallas kernels: 43.1 us -> 44.2 us  [the longest x1 42.2 us: per_device(): pl.pallas_call(kernel, out_shape=(jax.ShapeDtypeStruct((CTX, OWN, ROWS),...]
where the time goes in v4:
time: 45 us; the launch traced here: 44.8 us
  Pallas kernels  44.2 us (98%)
  between operations  0.64 us (1%)
    pallas_call x1, Pallas kernels, per_device(): pl.pallas_call(kernel, out_shape=(jax.ShapeDtypeStruct((CTX, OWN, ROWS),...  42.2 us
    pallas_call x1, Pallas kernels, per_device(): pl.pallas_call(turn, out_shape=(shape, shape), in_specs=[vmem] * 2, out_s...  1.96 us

profile of v4, /device:TPU:1, one launch (start us, length us, event | category | flops | bytes accessed | tf_op | source)
XLA Modules:
  0.0 44.8 jit_solution(13661579173047794621)
XLA Ops:
  0.6 42.2 %shard_map.104 = (bf16[32,32,128]{2,1,0:T(8,128)(2,1)}, bf16[16,64,128]{2,1,0:T(8,128)(2,1)}) custom-call(s32[1,128]{1,0:T(1,128)} %bitcast.10, s32[1,128]{1,0:T(1,128)} %bitcast.11, bf16[512,1024]{1,0:T(8,128)(2,1)} %table_hbm.1, f32[1,1024]{1,0:T(1,128)} %bitcast.9, bf16[128,1024]{1,0:T(8,128)(2,1)} %gate_hbm.1, bf16[128,1024]{1,0:T(8,128)(2,1)} %key_hbm.1, ...), custom_call_target="tpu_custom_call" | custom-call | tf_op jit(solution)/shard_map/pallas_call | solution.py:410
  42.9 2.0 %shard_map.105 = (bf16[128,1024]{1,0:T(8,128)(2,1)}, bf16[128,1024]{1,0:T(8,128)(2,1)}) custom-call(bf16[1024,128]{1,0:T(8,128)(2,1)} %bitcast.6, bf16[1024,128]{1,0:T(8,128)(2,1)} %bitcast.7), custom_call_target="tpu_custom_call" | custom-call | tf_op jit(solution)/shard_map/pallas_call | solution.py:464

commit v5 on v4

--- a/solution.py
+++ b/solution.py
@@ -160,18 +160,6 @@
     source_out[...] = product.T.astype(BF16).reshape(CTX, OWN, ROWS)
     source_in[me] = source_out[me]
 
-    pl.semaphore_wait(barrier, CTX - 1 + CH - 1)
-
-    @pl.loop(1, CTX)
-    def _(r):
-        to = lax.rem(me + r, CTX)
-        remote(meta_out.at[to], meta_in.at[me], META, {"ctx": to}).start()
-
-    @pl.loop(1, CTX)
-    def _(r):
-        to = lax.rem(me + r, CTX)
-        remote(source_out.at[to], source_in.at[me], SOURCE, {"ctx": to}).start()
-
     by_lane = jnp.zeros((VOCAB, 128), F32)
     for tile in range(WIDTH // 128):
         part = table_ref[:, tile * 128 : (tile + 1) * 128].astype(F32)
@@ -180,13 +168,27 @@
     ones = jnp.ones((8, 128), BF16)
     squares[my_ch] = nt_dot(ones, high) + nt_dot(ones, low)
 
+    loads[6].wait()
+    gate_out[...] = gate_ref[...].astype(F32).T.astype(BF16).reshape(CTX, OWN, ROWS)
+    gate_in[me] = gate_out[me]
+
+    values_t[64:80, :] = jnp.ones((16, CTX * ROWS), BF16)
+
+    pl.semaphore_wait(barrier, CTX - 1 + CH - 1)
+
     for r in range(1, CH):
         to = lax.rem(my_ch + r, CH)
         remote(squares.at[my_ch], squares.at[my_ch], SQUARES, {"ch": to}).start()
 
-    loads[6].wait()
-    gate_out[...] = gate_ref[...].astype(F32).T.astype(BF16).reshape(CTX, OWN, ROWS)
-    gate_in[me] = gate_out[me]
+    @pl.loop(1, CTX)
+    def _(r):
+        to = lax.rem(me + r, CTX)
+        remote(source_out.at[to], source_in.at[me], SOURCE, {"ctx": to}).start()
+
+    @pl.loop(1, CTX)
+    def _(r):
+        to = lax.rem(me + r, CTX)
+        remote(meta_out.at[to], meta_in.at[me], META, {"ctx": to}).start()
 
     @pl.loop(1, CTX)
     def _(r):
@@ -206,8 +208,6 @@
         remote(
             attn_query_ref.at[:, head], my_queries, QUERY, {"ctx": to}, query_recv.at[r]
         ).start()
-
-    values_t[64:80, :] = jnp.ones((16, CTX * ROWS), BF16)
 
     wait_in(meta_in.at[pl.ds(0, CTX - 1)], META)
     down = lax.broadcasted_iota(jnp.int32, (ROWS, ROWS), 0)

time: 45 us -> 44.6 us (level)
  the two profiles are of different devices: /device:TPU:1 before, /device:TPU:22 now
where the time goes in v5:
time: 44.6 us; the launch traced here: 44.4 us
  Pallas kernels  43.8 us (98%)
  between operations  0.64 us (1%)
    pallas_call x1, Pallas kernels, per_device(): pl.pallas_call(kernel, out_shape=(jax.ShapeDtypeStruct((CTX, OWN, ROWS),...  41.8 us
    pallas_call x1, Pallas kernels, per_device(): pl.pallas_call(turn, out_shape=(shape, shape), in_specs=[vmem] * 2, out_s...  1.96 us

profile of v5, /device:TPU:22, one launch (start us, length us, event | category | flops | bytes accessed | tf_op | source)
XLA Modules:
  0.0 44.4 jit_solution(6665604767137050128)
XLA Ops:
  0.6 41.8 %shard_map.104 = (bf16[32,32,128]{2,1,0:T(8,128)(2,1)}, bf16[16,64,128]{2,1,0:T(8,128)(2,1)}) custom-call(s32[1,128]{1,0:T(1,128)} %bitcast.10, s32[1,128]{1,0:T(1,128)} %bitcast.11, bf16[512,1024]{1,0:T(8,128)(2,1)} %table_hbm.1, f32[1,1024]{1,0:T(1,128)} %bitcast.9, bf16[128,1024]{1,0:T(8,128)(2,1)} %gate_hbm.1, bf16[128,1024]{1,0:T(8,128)(2,1)} %key_hbm.1, ...), custom_call_target="tpu_custom_call" | custom-call | tf_op jit(solution)/shard_map/pallas_call | solution.py:410
  42.4 2.0 %shard_map.105 = (bf16[128,1024]{1,0:T(8,128)(2,1)}, bf16[128,1024]{1,0:T(8,128)(2,1)}) custom-call(bf16[1024,128]{1,0:T(8,128)(2,1)} %bitcast.6, bf16[1024,128]{1,0:T(8,128)(2,1)} %bitcast.7), custom_call_target="tpu_custom_call" | custom-call | tf_op jit(solution)/shard_map/pallas_call | solution.py:464

commit v6 on v5

--- a/solution.py
+++ b/solution.py
@@ -356,13 +356,11 @@
             arrived = query_recv.at[lax.rem(mine + 16 - 2 * u - at, 16)]
             pltpu.make_async_copy(block, block, arrived).wait()
 
-        @pl.when(u < 2)
-        def _():
-            attend(u, 0, 8, 0)
-
-        @pl.when((u >= 2) & (u < 4))
-        def _():
-            attend(u, 0, 16, 8)
+        for early in range(4):
+
+            @pl.when(u == early)
+            def _():
+                attend(u, 0, 4 * early + 4, 4 * early)
 
         @pl.when(u >= 4)
         def _():
@@ -389,8 +387,8 @@
 
 
 def turn(home_ref, attn_ref, hyena_out_ref, attn_out_ref):
-    hyena_out_ref[...] = home_ref[...].astype(F32).T.astype(BF16)
-    attn_out_ref[...] = attn_ref[...].astype(F32).T.astype(BF16)
+    hyena_out_ref[...] = home_ref[...].T
+    attn_out_ref[...] = attn_ref[...].T
 
 
 def per_device(

time: 44.6 us -> 44.2 us (level)
  the two profiles are of different devices: /device:TPU:22 before, /device:TPU:1 now
where the time goes in v6:
time: 44.2 us; the launch traced here: 43.5 us
  Pallas kernels  42.8 us (97%)
  between operations  0.64 us (1%)
    pallas_call x1, Pallas kernels, per_device(): pl.pallas_call(kernel, out_shape=(jax.ShapeDtypeStruct((CTX, OWN, ROWS),...  40.9 us
    pallas_call x1, Pallas kernels, per_device(): pl.pallas_call(turn, out_shape=(shape, shape), in_specs=[vmem] * 2, out_s...  1.94 us

profile of v6, /device:TPU:1, one launch (start us, length us, event | category | flops | bytes accessed | tf_op | source)
XLA Modules:
  0.0 43.5 jit_solution(6306844373750243884)
XLA Ops:
  0.6 40.9 %shard_map.104 = (bf16[32,32,128]{2,1,0:T(8,128)(2,1)}, bf16[16,64,128]{2,1,0:T(8,128)(2,1)}) custom-call(s32[1,128]{1,0:T(1,128)} %bitcast.10, s32[1,128]{1,0:T(1,128)} %bitcast.11, bf16[512,1024]{1,0:T(8,128)(2,1)} %table_hbm.1, f32[1,1024]{1,0:T(1,128)} %bitcast.9, bf16[128,1024]{1,0:T(8,128)(2,1)} %gate_hbm.1, bf16[128,1024]{1,0:T(8,128)(2,1)} %key_hbm.1, ...), custom_call_target="tpu_custom_call" | custom-call | tf_op jit(solution)/shard_map/pallas_call | solution.py:408
  41.5 1.9 %shard_map.105 = (bf16[128,1024]{1,0:T(8,128)(2,1)}, bf16[128,1024]{1,0:T(8,128)(2,1)}) custom-call(bf16[1024,128]{1,0:T(8,128)(2,1)} %bitcast.6, bf16[1024,128]{1,0:T(8,128)(2,1)} %bitcast.7), custom_call_target="tpu_custom_call" | custom-call | tf_op jit(solution)/shard_map/pallas_call | solution.py:462

commit v7 on v6

--- a/solution.py
+++ b/solution.py
@@ -157,7 +157,7 @@
     one_hot_t = (lax.broadcasted_iota(jnp.int32, (VOCAB, ROWS), 0) == ids_ref[...]).astype(F32)
     picked = nn_dot(one_hot_t.T.astype(BF16), table_ref[...])
     product = picked * key_ref[...].astype(F32) * gain_ref[...]
-    source_out[...] = product.T.astype(BF16).reshape(CTX, OWN, ROWS)
+    source_out[...] = product.astype(BF16).T.reshape(CTX, OWN, ROWS)
     source_in[me] = source_out[me]
 
     by_lane = jnp.zeros((VOCAB, 128), F32)
@@ -169,7 +169,7 @@
     squares[my_ch] = nt_dot(ones, high) + nt_dot(ones, low)
 
     loads[6].wait()
-    gate_out[...] = gate_ref[...].astype(F32).T.astype(BF16).reshape(CTX, OWN, ROWS)
+    gate_out[...] = gate_ref[...].T.reshape(CTX, OWN, ROWS)
     gate_in[me] = gate_out[me]
 
     values_t[64:80, :] = jnp.ones((16, CTX * ROWS), BF16)

time: 44.2 us -> 44.2 us (level)
  no operation moved by 1% of the time
where the time goes in v7:
time: 44.2 us; the launch traced here: 43.5 us
  Pallas kernels  42.8 us (97%)
  between operations  0.64 us (1%)
    pallas_call x1, Pallas kernels, per_device(): pl.pallas_call(kernel, out_shape=(jax.ShapeDtypeStruct((CTX, OWN, ROWS),...  40.9 us
    pallas_call x1, Pallas kernels, per_device(): pl.pallas_call(turn, out_shape=(shape, shape), in_specs=[vmem] * 2, out_s...  1.94 us

profile of v7, /device:TPU:1, one launch (start us, length us, event | category | flops | bytes accessed | tf_op | source)
XLA Modules:
  0.0 43.5 jit_solution(9248831960775818598)
XLA Ops:
  0.6 40.9 %shard_map.104 = (bf16[32,32,128]{2,1,0:T(8,128)(2,1)}, bf16[16,64,128]{2,1,0:T(8,128)(2,1)}) custom-call(s32[1,128]{1,0:T(1,128)} %bitcast.10, s32[1,128]{1,0:T(1,128)} %bitcast.11, bf16[512,1024]{1,0:T(8,128)(2,1)} %table_hbm.1, f32[1,1024]{1,0:T(1,128)} %bitcast.9, bf16[128,1024]{1,0:T(8,128)(2,1)} %gate_hbm.1, bf16[128,1024]{1,0:T(8,128)(2,1)} %key_hbm.1, ...), custom_call_target="tpu_custom_call" | custom-call | tf_op jit(solution)/shard_map/pallas_call | solution.py:408
  41.5 1.9 %shard_map.105 = (bf16[128,1024]{1,0:T(8,128)(2,1)}, bf16[128,1024]{1,0:T(8,128)(2,1)}) custom-call(bf16[1024,128]{1,0:T(8,128)(2,1)} %bitcast.6, bf16[1024,128]{1,0:T(8,128)(2,1)} %bitcast.7), custom_call_target="tpu_custom_call" | custom-call | tf_op jit(solution)/shard_map/pallas_call | solution.py:462
